TPU v7x, 256 devices: a whole 4x4x8 slice. The times are simulated.
256 devices in a mesh: row: 32 (over y, z), col: 8 (over x, core).
Axes of the slice: x: 4, y: 4, z: 8, core: 2. Of those that a mesh axis runs over, the one named last changes fastest.
Arguments:
- matrix: float32 [1, 32, 512, 4, 8, 512], P(None, 'row', None, None, 'col'), may hold values from -6 to 6
- pivots: int32 [2, 512], replicated, may hold values from 0 to 16383, as said below
- inverses: float32 [2, 512, 512], replicated, may hold values from -0.01171875 to 0.01171875
Outputs:
- factored: float32 [1, 32, 512, 4, 8, 512], P(None, 'row', None, None, 'col')
Inputs may be any that keep to these rules, and one draw needn't show every extreme that they name: pivots[k, t] is either 512 * k + t itself or a row at or after 512 * (k + 1); the entries of one panel's list are distinct; position 0 of each panel keeps its own row, position 1 takes row 16383 and position 2 takes row 512 * (k + 1).
All inputs are finite; a program needn't handle non-finite values.
Results may differ from a plain program's by a relative error of at most 0.00011.
Values sent between devices are 32-bit elements; how exact they have to be, the bound alone decides.
No kernel may reach another device: no remote copies, remote signals or barrier semaphores. Data moves between devices by JAX's collectives and lax.ppermute only.
A program may use at most 128 MiB of HBM per device.

v0:
```python
import functools

import jax
import jax.numpy as jnp
from jax import lax
from jax.experimental import pallas as pl
from jax.experimental.pallas import tpu as pltpu
from jax.sharding import Mesh, PartitionSpec as P

Y, Z, X, CORE = 4, 8, 4, 2
NB = 512
LANES = 128
SUB = 16
SLOTS = 8
CAP = 4 * SLOTS
KEEP = 32
REST = 128 - KEEP
WAVE = 4 * KEEP + REST
ROW = ("y", "z")
COL = ("x", "core")
HIGHEST = lax.Precision.HIGHEST
F32 = jnp.float32
I32 = jnp.int32


def from_root(x, axis, root):
    mine = lax.axis_index(axis) == root
    return lax.psum(jnp.where(mine, x, jnp.zeros_like(x)), axis)


def general(work, pivots, inverses):
    row_index = lax.axis_index(ROW)
    col_index = lax.axis_index(COL)
    work = work.reshape(NB, SUB * LANES)
    row_ids = row_index * NB + jnp.arange(NB, dtype=I32)
    col_ids = (
        (jnp.arange(4, dtype=I32)[:, None] * 8 + col_index) * NB
        + jnp.arange(NB, dtype=I32)[None, :]
    ).reshape(-1)
    for panel in range(2):
        after_row = (panel + 1) * NB
        targets = pivots[panel]
        held = targets // NB == row_index
        local_row = targets % NB
        picked = jnp.where(held[:, None], jnp.take(work, local_row, axis=0), 0.0)
        u_rows = lax.psum(picked, ROW)
        displaced = from_root(work, ROW, panel)
        dest_row = jnp.where(held, local_row, NB)
        work = work.at[dest_row].set(displaced, mode="drop")
        work = jnp.where(row_index == panel, u_rows, work)
        panel_cols = work[:, :NB]
        product = jnp.dot(panel_cols, inverses[panel], precision=HIGHEST)
        l_cols = from_root(product, COL, panel)
        below_mask = (row_ids >= after_row)[:, None]
        work = work.at[:, :NB].set(
            jnp.where(below_mask & (col_index == panel), l_cols, panel_cols)
        )
        update = jnp.dot(l_cols, u_rows, precision=HIGHEST)
        trail_mask = below_mask & (col_ids >= after_row)[None, :]
        work = jnp.where(trail_mask, work - update, work)
    return work.reshape(NB * SUB, LANES)


def ranks(key):
    t = jnp.arange(NB, dtype=I32)
    same = (key[:, None] == key[None, :]) & (t[None, :] < t[:, None])
    less = key[None, :] < key[:, None]
    rank = jnp.sum(same.astype(I32), axis=1)
    place = rank + jnp.sum(less.astype(I32), axis=1)
    return rank, place


def plan(pivots, y, z):
    r = y * Z + z
    t = jnp.arange(NB, dtype=I32)
    piv0, piv1 = pivots[0], pivots[1]
    meet = piv1[:, None] == piv0[None, :]
    src1 = jnp.where(jnp.any(meet, 1), jnp.sum(jnp.where(meet, t[None, :], 0), 1), piv1)
    src = (piv0, src1)
    in_home = piv0[:, None] == NB + t[None, :]
    moved = piv0[:, None] == piv1[None, :]
    dst0 = jnp.where(
        jnp.any(in_home, 1),
        jnp.sum(jnp.where(in_home, piv1[None, :], 0), 1),
        jnp.where(jnp.any(moved, 1), NB + jnp.sum(jnp.where(moved, t[None, :], 0), 1), piv0),
    )
    taken = (NB + t)[:, None] == piv0[None, :]
    dst1 = jnp.where(jnp.any(taken, 1), jnp.sum(jnp.where(taken, t[None, :], 0), 1), piv1)
    dst = (dst0, dst1)

    k_rank, k_place, k_key = [], [], []
    h_rank, h_place, h_key = [], [], []
    for h in range(2):
        own = h * NB + t
        stay = src[h] == own
        key = jnp.where(stay, -1, src[h] // NB)
        rank, place = ranks(key)
        k_key.append(key), k_rank.append(rank), k_place.append(place)
        away = dst[h] >= 2 * NB
        hkey = jnp.where(stay, -1, jnp.where(away, dst[h] // NB, 32))
        rank, place = ranks(hkey)
        h_key.append(hkey), h_rank.append(rank), h_place.append(place)
    over = jnp.zeros((), jnp.bool_)
    for h in range(2):
        over = over | jnp.any((k_key[h] >= 0) & (k_rank[h] >= CAP))
        over = over | jnp.any((h_key[h] >= 0) & (h_key[h] < 32) & (h_rank[h] >= CAP))
        over = over | jnp.any((h_key[h] < 0) & (h_rank[h] >= 4 * KEEP))

    def spot(place):
        return (place % 4) * 128 + place // 4

    mine = z % 2
    pick = lambda pair: jnp.where(mine == 0, pair[0], pair[1])
    home_spot = spot(pick(h_place))
    home_list = jnp.sum(jnp.where(home_spot[None, :] == t[:, None], t[None, :], 0), 1)
    e = jnp.arange(4 * SLOTS, dtype=I32)
    give = []
    for h in range(2):
        code = jnp.where(k_key[h] == r, (k_place[h] % 4) * SLOTS + k_rank[h] // 4, -1)
        code = jnp.where(k_rank[h] < CAP, code, -1)
        give.append(jnp.sum(jnp.where(code[None, :] == e[:, None], (src[h] % NB)[None, :], 0), 1))
    give_list = jnp.concatenate(give)
    place, key, rank = pick(k_place), pick(k_key), pick(k_rank)
    code = jnp.where(key < 0, -1, jnp.minimum(key * SLOTS + rank // 4, 32 * SLOTS - 1))
    i = jnp.arange(128, dtype=I32) * 4 + y
    slice_list = jnp.sum(jnp.where(place[None, :] == i[:, None], code[None, :], 0), 1)
    place, key, rank = pick(h_place), pick(h_key), pick(h_rank)
    ok = (place % 4 == y) & (key >= 0) & (key < 32) & (rank < CAP)
    code = jnp.where(ok, key * SLOTS + rank // 4, -1)
    e = jnp.arange(32 * SLOTS, dtype=I32)
    away_list = jnp.sum(jnp.where(code[None, :] == e[:, None], (place // 4)[None, :], 0), 1)
    e = jnp.arange(CAP, dtype=I32)
    to_row, from_y = [], []
    for h in range(2):
        hit = ((h_key[h] == r)[None, :]) & (h_rank[h][None, :] == e[:, None])
        to_row.append(jnp.sum(jnp.where(hit, (dst[h] % NB + 1)[None, :], 0), 1) - 1)
        from_y.append(jnp.sum(jnp.where(hit, (h_place[h] % 4)[None, :], 0), 1))
    to_row, from_y = jnp.concatenate(to_row), jnp.concatenate(from_y)
    hot = [jnp.broadcast_to(spot(k_place[h])[:, None], (NB, LANES)) for h in range(2)]
    return home_list, give_list, slice_list, away_list, to_row, from_y, hot, over


VMEM = pl.BlockSpec(memory_space=pltpu.VMEM)
SMEM = pl.BlockSpec(memory_space=pltpu.SMEM)


def call(kernel, name, out_shape, in_specs, mib, us, scratch=(), alias=None, out_specs=None):
    return pl.pallas_call(
        kernel,
        out_shape=out_shape,
        in_specs=in_specs,
        out_specs=[VMEM] * len(out_shape) if out_specs is None else out_specs,
        scratch_shapes=list(scratch),
        input_output_aliases=alias or {},
        compiler_params=pltpu.CompilerParams(vmem_limit_bytes=mib << 20),
        cost_estimate=pl.CostEstimate(flops=0, bytes_accessed=us * 3_000_000, transcendentals=0),
        name=name,
    )


def shaped(*shape, dtype=F32):
    return jax.ShapeDtypeStruct(shape, dtype)


def pack_kernel(home_ref, give_ref, x_ref, h_ref, rest_ref, g_ref):
    def give(n, _):
        row = give_ref[n] * SUB
        h, y, s = n // (4 * SLOTS), (n // SLOTS) % 4, n % SLOTS
        for k in range(4):
            g_ref[pl.ds(((y * 8 + 2 * k + h) * SLOTS + s) * 4, 4), :] = x_ref[pl.ds(row + k, 4, stride=4), :]
        return 0

    def keep(n, _):
        y, i = n // KEEP, n % KEEP
        row = home_ref[y * 128 + i] * SUB
        for k in range(4):
            h_ref[pl.ds((y * 4 + k) * WAVE + i * 4, 4), :] = x_ref[pl.ds(row + k, 4, stride=4), :]
        return 0

    def rest(n, _):
        y, i = n // REST, n % REST
        row = home_ref[y * 128 + KEEP + i] * SUB
        for k in range(4):
            h_ref[pl.ds((y * 4 + k) * WAVE + 4 * KEEP + i, 1), :] = x_ref[pl.ds(row + k, 1), :]
            rest_ref[pl.ds(((y * 4 + k) * REST + i) * 3, 3), :] = x_ref[pl.ds(row + 4 + k, 3, stride=4), :]
        return 0

    lax.fori_loop(0, 8 * SLOTS, give, 0, unroll=8)
    lax.fori_loop(0, 4 * KEEP, keep, 0, unroll=8)
    lax.fori_loop(0, 4 * REST, rest, 0, unroll=8)


def pack(home_list, give_list, x):
    out = [shaped(16 * WAVE, LANES), shaped(16 * REST * 3, LANES), shaped(32 * SLOTS * 4, LANES)]
    return call(pack_kernel, "pack", out, [SMEM, SMEM, VMEM], 24, 8)(home_list, give_list, x)


def slice_kernel(slice_ref, hs_ref, recv_ref, s_ref):
    def one(i, _):
        code = slice_ref[i]
        theirs = recv_ref[pl.ds(jnp.maximum(code, 0) * 4, 4), :]
        here = hs_ref[pl.ds(jnp.minimum(i, KEEP - 1) * 4, 4), :]
        s_ref[pl.ds(i, 4, stride=128), :] = jnp.where(code < 0, here, theirs)
        return 0

    lax.fori_loop(0, 128, one, 0, unroll=8)


def make_slice(slice_list, hs, recv):
    return call(slice_kernel, "pivot_slice", [shaped(512, LANES)], [SMEM, VMEM, VMEM], 16, 2)(slice_list, hs, recv)[0]


def away_kernel(away_ref, keep_ref, d_ref):
    def away(n, _):
        i = away_ref[n]
        d_ref[pl.ds(n, 1), :] = keep_ref[pl.ds(jnp.where(i < KEEP, i * 4, i + 3 * KEEP), 1), :]
        return 0

    lax.fori_loop(0, 32 * SLOTS, away, 0, unroll=8)


def make_away(away_list, keep):
    out = [shaped(32 * SLOTS, LANES)]
    return call(away_kernel, "away_first", out, [SMEM, VMEM], 16, 1)(away_list, keep)[0]


def away_rest_kernel(away_ref, keep_ref, rest_ref, d_ref):
    def away(n, _):
        i = away_ref[n]
        a = keep_ref[pl.ds(jnp.minimum(i, KEEP - 1) * 4 + 1, 3), :]
        b = rest_ref[pl.ds(jnp.maximum(i - KEEP, 0) * 3, 3), :]
        d_ref[pl.ds(n * 3, 3), :] = jnp.where(i < KEEP, a, b)
        return 0

    lax.fori_loop(0, 32 * SLOTS, away, 0, unroll=8)


def make_away_rest(away_list, keep, rest):
    out = [shaped(32 * SLOTS * 3, LANES)]
    return call(away_rest_kernel, "away_rest", out, [SMEM, VMEM, VMEM], 16, 2)(away_list, keep, rest)[0]


def patch_kernel(row_ref, y_ref, x_ref, first_ref, rest_ref, o_ref):
    o_ref[...] = x_ref[...]

    def one(n, _):
        row, y = row_ref[n], y_ref[n]
        h, s = n // CAP, (n % CAP) // 4

        @pl.when(row >= 0)
        def _():
            o_ref[pl.ds(row * SUB, 4), :] = first_ref[pl.ds((y * 8 + h) * SLOTS + s, 4, stride=2 * SLOTS), :]
            for k in range(4):
                piece = rest_ref[pl.ds(((y * 8 + 2 * k + h) * SLOTS + s) * 3, 3), :]
                o_ref[pl.ds(row * SUB + 4 + k, 3, stride=4), :] = piece

        return 0

    lax.fori_loop(0, 2 * CAP, one, 0)


def patch(to_row, from_y, x, first, rest):
    out = [shaped(NB * SUB, LANES)]
    return call(patch_kernel, "patch_rows", out, [SMEM] * 2 + [VMEM] * 3, 24, 4)(to_row, from_y, x, first, rest)[0]


def split(v):
    hi = v.astype(jnp.bfloat16)
    return hi, (v - hi.astype(F32)).astype(jnp.bfloat16)


def dot3(a, b):
    dot = functools.partial(jnp.dot, preferred_element_type=F32)
    return dot(a[0], b[0]) + dot(a[0], b[1]) + dot(a[1], b[0])


OFF_X = (0, -1, 1, 2)


def factor_kernel(
    info_ref, row_ref, y_ref, own_ref, swap_ref, late_ref, late_swap, piece_ref, piece_swap,
    inv0_ref, inv1_ref, spot0_ref, spot1_ref,
    m_ref, sp_ref, a0, a1, u01, p0, lin0, lin1,
):
    r, c, x, core = info_ref[4], info_ref[5], info_ref[6], info_ref[7]
    first = core == 0
    own, other = own_ref[...], swap_ref[...]
    lin0[...] = jnp.where(first, own, other)
    lin1[...] = jnp.where(first, other, own)

    def one(n, _):
        row, y = row_ref[n], y_ref[n]
        h, s = n // CAP, (n % CAP) // 4

        @pl.when(row >= 0)
        def _():
            at = pl.ds((y * 8 + h) * SLOTS + s, 4, stride=2 * SLOTS)
            own, other = late_ref[at, :], late_swap[at, :]
            lin0[pl.ds(row * 4, 4), :] = jnp.where(first, own, other)
            lin1[pl.ds(row * 4, 4), :] = jnp.where(first, other, own)

        return 0

    lax.fori_loop(0, 2 * CAP, one, 0)
    for j in range(4):
        cols = slice(j * 128, (j + 1) * 128)
        a0[:, cols] = lin0[pl.ds(j, NB, stride=4), :]
        a1[:, cols] = lin1[pl.ds(j, NB, stride=4), :]
    for m, dx in enumerate(OFF_X):
        for ref, cc in ((piece_ref, core), (piece_swap, 1 - core)):
            part = lax.rem(x + (dx + 4), 4) * 2 + cc
            for yy in range(4):
                rows = pl.ds(pl.multiple_of(yy * 128 + part * 16, 16), 16)
                for k in range(4):
                    cols = slice(k * 128, (k + 1) * 128)
                    u01[rows, cols] = ref[m, yy * 8 + 2 * k]
                    p0[rows, cols] = ref[m, yy * 8 + 2 * k + 1]

    dot = functools.partial(jnp.dot, preferred_element_type=F32)
    place = lax.broadcasted_iota(I32, (NB, NB), 1)
    hot0 = jnp.where(spot0_ref[:, :1] == place, 1.0, 0.0)
    hot1 = jnp.where(spot1_ref[:, :1] == place, 1.0, 0.0)
    inv0, inv1 = split(inv0_ref[...]), split(inv1_ref[...])

    def turned(inv, hot):
        hot = hot.astype(jnp.bfloat16)
        return tuple(dot(v, hot).astype(jnp.bfloat16) for v in inv)

    inv0p, inv1p = turned(inv0, hot0), turned(inv1, hot1)
    p0s = split(p0[...])

    @pl.when(r == 1)
    def _():
        at = hot1.astype(jnp.bfloat16)
        a0[...] = dot(at, p0s[0]) + dot(at, p0s[1])

    def put(at, v):
        hi, lo = split(v)
        m_ref[:NB, at : at + NB] = hi
        m_ref[NB:, at : at + NB] = lo

    l0 = dot3(split(a0[...]), inv0p)
    a1[...] = a1[...] - dot3(split(l0), split(u01[...]))
    l1 = dot3(split(a1[...]), inv1p)
    lp0 = dot3(p0s, inv0p)
    m0 = jnp.where(r == 1, l0, l0 - dot3(split(l1), split(lp0)))
    put(0, jnp.where(r == 0, -hot0, m0))
    put(NB, jnp.where(r == 0, 0.0, jnp.where(r == 1, -hot1, l1)))

    @pl.when(c == 0)
    def _():
        sp_ref[...] = dot3(split(a0[...]), inv0)

    @pl.when(c != 0)
    def _():
        sp_ref[...] = dot3(split(a1[...]), inv1)


def factors(info, to_row, from_y, *rest):
    out = [shaped(2 * NB, 2 * NB, dtype=jnp.bfloat16), shaped(NB, NB)]
    scratch = [pltpu.VMEM((NB, NB), F32)] * 4 + [pltpu.VMEM((NB * 4, LANES), F32)] * 2
    specs = [SMEM] * 3 + [VMEM] * len(rest)
    return call(factor_kernel, "factors", out, specs, 48, 12, scratch)(info, to_row, from_y, *rest)


OFF_Y = (0, -1, 1, 2)


def update_kernel(info_ref, x_ref, m_ref, sp_ref, u_ref, o_ref, uh, ul):
    i = pl.program_id(0)
    y, home, special = info_ref[0], info_ref[2], info_ref[3]
    x2, o2 = x_ref.reshape(NB * 8, LANES), o_ref.reshape(NB * 8, LANES)
    for m, dy in enumerate(OFF_Y):
        at = lax.rem(y + (dy + 4), 4) * 128
        for zz in range(4):
            rows = pl.ds(pl.multiple_of((zz % 2) * 512 + at, 128), 128)
            cols = slice(zz // 2 * 128, zz // 2 * 128 + 128)
            uh[rows, cols], ul[rows, cols] = split(u_ref[zz, m, 0])
    dot = functools.partial(jnp.dot, preferred_element_type=F32)
    both = dot(m_ref[...], uh[...])
    acc = both[:NB] + both[NB:] + dot(m_ref[:NB, :], ul[...])
    for s in range(2):
        j = 2 * lax.rem(i, 4) + s
        base = x2[pl.ds(j, NB, stride=8), :]
        new = jnp.where(home > 0, 0.0, base) - acc[:, s * 128 : (s + 1) * 128]
        put = sp_ref[:, pl.ds(pl.multiple_of(lax.rem(j, 4) * 128, 128), 128)]
        o2[pl.ds(j, NB, stride=8), :] = jnp.where((special > 0) & (i < 2), put, new)


def update(info, x, m, special, rows):
    half = pl.BlockSpec((NB, 8, LANES), lambda i: (0, i // 4, 0))
    whole = pl.BlockSpec((2 * NB, 2 * NB), lambda i: (0, 0))
    tile = pl.BlockSpec((4, 4, 1, 128, 128), lambda i: (i % 2, 0, i // 2, 0, 0))
    return pl.pallas_call(
        update_kernel,
        out_shape=shaped(NB, SUB, LANES),
        grid=(8,),
        in_specs=[SMEM, half, whole, pl.BlockSpec((NB, NB), lambda i: (0, 0)), tile],
        out_specs=half,
        scratch_shapes=[pltpu.VMEM((1024, 256), jnp.bfloat16)] * 2,
        compiler_params=pltpu.CompilerParams(vmem_limit_bytes=60 << 20),
        cost_estimate=pl.CostEstimate(flops=0, bytes_accessed=30_000_000, transcendentals=0),
        name="update",
    )(info, x, m, special, rows)


def join_kernel(count, *refs):
    parts, outs = refs[:-count], refs[-count:]
    each = len(parts) // count
    for n, ref in enumerate(parts):
        outs[n // each][n % each] = ref[...]


def join(parts, count=1):
    out = [shaped(len(parts) // count, *parts[0].shape)] * count
    return call(functools.partial(join_kernel, count), "join", out, [VMEM] * len(parts), 16, 1)(*parts)


def shift(v, axis, step):
    n = {"y": Y, "z": Z, "x": X, "core": CORE}[axis]
    return lax.ppermute(v, axis, [(i, (i + step) % n) for i in range(n)])


def tie(*values):
    return lax.optimization_barrier(values)


def scatter_y(blocks):
    go = lambda b: lax.ppermute(blocks[b], ROW, [(h, b * Z + h) for h in range(2)])
    return go(2), go(1), go(3)


def scatter_z(block):
    out = []
    for k in (2, 1, 3):
        pairs = [(i * Z + h, i * Z + 2 * k + h) for i in range(Y) for h in range(2)]
        out.append(lax.ppermute(block[k], ROW, pairs))
    return out


def body(matrix, pivots, inverses):
    y, z = lax.axis_index("y"), lax.axis_index("z")
    x, core = lax.axis_index("x"), lax.axis_index("core")
    r = y * Z + z
    c = x * CORE + core
    work = matrix.reshape(NB * SUB, LANES)
    panel = work.reshape(NB, SUB, LANES)[:, :4].reshape(NB * 4, LANES)
    panel = jnp.where(x == 0, panel, 0.0)
    home_list, give_list, slice_list, away_list, to_row, from_y, hot, over = plan(pivots, y, z)
    is_special = ((c == 0) & (r >= 1)) | ((c == 1) & (r >= 2))
    info = jnp.stack([y, z, (r < 2).astype(I32), is_special.astype(I32), r, c, x, core])
    inv0, inv1 = inverses[0], inverses[1]

    keep, rest, send = pack(home_list, give_list, work)
    keep, rest = keep.reshape(4, 4, WAVE, LANES), rest.reshape(4, 4, REST * 3, LANES)
    keep_y = scatter_y(keep)
    recv = lax.all_to_all(send.reshape(32, 4 * SLOTS, LANES), ROW, 0, 0)
    keep = jnp.where(y == 0, keep[0], sum(keep_y))
    keep_z = scatter_z(keep)
    keep, panel, to_row, from_y, spot0, spot1, *keep_z = tie(keep, panel, to_row, from_y, *hot, *keep_z)
    keep = jnp.where(z < 2, keep[0], sum(keep_z))
    panel = lax.psum(panel, "x")
    mine = make_slice(slice_list, keep, recv.reshape(-1, LANES)).reshape(4, 128, LANES)

    parts = [shift(mine, "y", n) for n in (1, -1, 2)]
    away = make_away(away_list, keep)
    away, rest, *parts = tie(away, rest, *parts)
    rows = lax.all_gather(join([mine] + parts)[0], "z", axis=0)

    recv_first = lax.all_to_all(away.reshape(32, SLOTS, LANES), ROW, 0, 0)
    rest_y = scatter_y(rest)
    piece = lax.all_to_all(mine[0].reshape(8, 16, LANES), COL, 0, 0)
    piece, recv_first, *rest_y = tie(piece, recv_first, *rest_y)
    rest = jnp.where(y == 0, rest[0], sum(rest_y))
    rest_z = scatter_z(rest)
    piece = lax.dynamic_slice_in_dim(piece, 1 - z % 2, 1, 0)
    piece = lax.all_to_all(jnp.broadcast_to(piece, (32, 16, LANES)), ROW, 0, 0)
    late = recv_first.reshape(-1, LANES)
    late_x = [lax.ppermute(late, "x", [(0, b)]) for b in (2, 1, 3)]
    piece, la, lb, lc, *rest_z = tie(piece, *late_x, *rest_z)
    late = jnp.where(x == 0, late, la + lb + lc)
    late_swap = shift(late, "core", 1)
    pieces = [shift(piece, "x", n) for n in (1, -1, 2)]
    swap = shift(panel, "core", 1)
    rest = jnp.where(z < 2, rest[0], sum(rest_z))
    away = make_away_rest(away_list, keep, rest)
    recv_rest = lax.all_to_all(away.reshape(32, SLOTS * 3, LANES), ROW, 0, 0)
    recv_rest, late_swap, swap, *pieces = tie(recv_rest, late_swap, swap, *pieces)
    piece = join([piece] + pieces)[0]
    piece_swap = shift(piece, "core", 1)
    base = patch(to_row, from_y, work, recv_first.reshape(-1, LANES), recv_rest.reshape(-1, LANES))
    m, special = factors(
        info, to_row, from_y, panel, swap, late, late_swap, piece, piece_swap, inv0, inv1, spot0, spot1,
    )
    out = update(info, base.reshape(NB, SUB, LANES), m, special, rows)
    out = out.reshape(NB * SUB, LANES)
    out = lax.cond(over, lambda o: general(work, pivots, inverses), lambda o: o, out)
    return out.reshape(matrix.shape)


def solution(mesh):
    grid = Mesh(mesh.devices.reshape(Y, Z, X, CORE), ("y", "z", "x", "core"))
    placed = (P(None, ROW, None, None, COL, None), P(), P())
    return jax.shard_map(
        body,
        mesh=grid,
        in_specs=placed,
        out_specs=P(None, ROW, None, None, COL, None),
        check_vma=False,
    )
```

profile of v0, /device:TPU:33, one launch (start us, length us, event | category | flops | bytes accessed | tf_op | source)
XLA Modules:
  0.0 237.0 jit_solution(5895026807956195760)
XLA Ops:
  14.0 9.6 %pack.1 = (f32[3584,128]{1,0:T(8,128)S(1)}, f32[4608,128]{1,0:T(8,128)S(1)}, f32[1024,128]{1,0:T(8,128)}) custom-call(s32[512]{0:T(512)S(1)} %select_reduce_fusion.home_ref, s32[64]{0:T(128)S(1)} %pad_add_fusion.give_ref, f32[8192,128]{1,0:T(8,128)} %bitcast.142), custom_call_target="tpu_custom_call" | custom-call | bytes 24000000 | tf_op jit(solution)/shard_map/pack/pallas_call | solution.py:195
  24.9 5.6 %collective-permute-start = (f32[4,224,128]{2,1,0:T(8,128)}, f32[4,224,128]{2,1,0:T(8,128)}, u32[]{:S(2)}, u32[]{:S(2)}) collective-permute-start(f32[4,224,128]{2,1,0:T(8,128)} %bitcast.36), channel_id=1, source_target_pairs={{0,128},{8,136},{1,129},{9,137},{2,130},{10,138},{3,131},{11,139},... | collective-permute-start | bytes 1376264 | tf_op jit(solution)/shard_map/ppermute | solution.py:429
  30.5 2.1 collective-permute-start.1
  32.6 2.1 collective-permute-start.2
  34.6 5.4 %all-to-all-start = ((f32[32,32,128]{2,1,0:T(8,128)}), f32[32,32,128]{2,1,0:T(8,128)S(1)}, u32[]{:S(2)}, u32[]{:S(2)}) async-start(f32[32,32,128]{2,1,0:T(8,128)} %bitcast.48), calls=%async_computation | async-start | bytes 1048576 | tf_op jit(solution)/shard_map/all_to_all | solution.py:457
  40.4 2.7 %slice_select_fusion = f32[512,4,128]{2,1,0:T(4,128)} fusion(f32[512,16,128]{2,1,0:T(8,128)} %bitcast.143, pred[]{:T(512)S(6)} %eq.411), kind=kLoop, calls=%fused_computation.88 | loop fusion | flops 262144 | bytes 2097153 | tf_op jit(solution)/shard_map/jit(_where)/select_n | solution.py:448
  43.1 10.2 %collective-permute-done.1 = f32[4,224,128]{2,1,0:T(8,128)} collective-permute-done((f32[4,224,128]{2,1,0:T(8,128)}, f32[4,224,128]{2,1,0:T(8,128)}, u32[]{:S(2)}, u32[]{:S(2)}) %collective-permute-start.1) | collective-permute-done | bytes 458784 | tf_op jit(solution)/shard_map/ppermute | solution.py:429
  53.3 1.5 add_select_fusion.4
  54.9 1.3 collective-permute-start.3
  56.2 1.3 collective-permute-start.4
  57.5 1.3 collective-permute-start.5
  58.9 4.0 %collective-permute-done.4 = f32[224,128]{1,0:T(8,128)S(1)} collective-permute-done((f32[224,128]{1,0:T(8,128)S(1)}, f32[224,128]{1,0:T(8,128)S(1)}, u32[]{:S(2)}, u32[]{:S(2)}) %collective-permute-start.4) | collective-permute-done | bytes 114720 | tf_op jit(solution)/shard_map/ppermute | solution.py:437
  67.1 3.0 %collective-permute-start.6 = (f32[4,128,128]{2,1,0:T(8,128)S(1)}, f32[4,128,128]{2,1,0:T(8,128)S(1)}, u32[]{:S(2)}, u32[]{:S(2)}) collective-permute-start(f32[4,128,128]{2,1,0:T(8,128)S(1)} %bitcast.131), channel_id=1, source_target_pairs={{0,64},{64,128},{128,192},{192,0},{1,65},{65,129},{129,193},{193,1... | collective-permute-start | bytes 786440 | tf_op jit(solution)/shard_map/ppermute | solution.py:421
  70.1 1.9 collective-permute-start.8
  72.1 1.8 away_first.1
  73.9 6.9 %collective-permute-done.6.refs_1_ = f32[4,128,128]{2,1,0:T(8,128)S(1)} collective-permute-done((f32[4,128,128]{2,1,0:T(8,128)S(1)}, f32[4,128,128]{2,1,0:T(8,128)S(1)}, u32[]{:S(2)}, u32[]{:S(2)}) %collective-permute-start.6) | collective-permute-done | bytes 262176 | tf_op jit(solution)/shard_map/ppermute | solution.py:421
  83.2 5.2 %collective-permute-start.10 = (f32[4,288,128]{2,1,0:T(8,128)}, f32[4,288,128]{2,1,0:T(8,128)}, u32[]{:S(2)}, u32[]{:S(2)}) collective-permute-start(f32[4,288,128]{2,1,0:T(8,128)} %get-tuple-element.203), channel_id=1, source_target_pairs={{0,64},{8,72},{1,65},{9,73},{2,66},{10,74},{3,67},{11,75},{4,68},{... | collective-permute-start | bytes 1769480 | tf_op jit(solution)/shard_map/ppermute | solution.py:429
  88.4 3.3 %collective-permute-start.11 = (f32[4,288,128]{2,1,0:T(8,128)}, f32[4,288,128]{2,1,0:T(8,128)}, u32[]{:S(2)}, u32[]{:S(2)}) collective-permute-start(f32[4,288,128]{2,1,0:T(8,128)} %get-tuple-element.202), channel_id=1, source_target_pairs={{0,192},{8,200},{1,193},{9,201},{2,194},{10,202},{3,195},{11,203},... | collective-permute-start | bytes 1769480 | tf_op jit(solution)/shard_map/ppermute | solution.py:429
  91.7 2.2 collective-permute-start.9
  93.9 10.9 %all_to_all.25 = f32[8,16,128]{2,1,0:T(8,128)S(1)} all-to-all(f32[8,16,128]{2,1,0:T(8,128)S(1)} %bitcast.150), channel_id=1, replica_groups=mesh['y'=4,'z'=8,'x'=4,'core'=2] {'x','core'}, dimensions={0} | all-to-all | bytes 131072 | tf_op jit(solution)/shard_map/all_to_all | solution.py:472
  104.8 3.6 %all-to-all-start.2 = ((f32[32,8,128]{2,1,0:T(8,128)}), f32[32,8,128]{2,1,0:T(8,128)S(1)}, u32[]{:S(2)}, u32[]{:S(2)}) async-start(f32[32,8,128]{2,1,0:T(8,128)} %bitcast.56), calls=%async_computation.2 | async-start | bytes 262144 | tf_op jit(solution)/shard_map/all_to_all | solution.py:470
  108.4 10.1 %all-to-all-done.2 = f32[32,8,128]{2,1,0:T(8,128)S(1)} async-done(((f32[32,8,128]{2,1,0:T(8,128)}), f32[32,8,128]{2,1,0:T(8,128)S(1)}, u32[]{:S(2)}, u32[]{:S(2)}) %all-to-all-start.2) | async-done | bytes 131104 | tf_op jit(solution)/shard_map/all_to_all | solution.py:470
  118.6 3.9 %collective-permute-start.12 = (f32[256,128]{1,0:T(8,128)S(1)}, f32[256,128]{1,0:T(8,128)}, u32[]{:S(2)}, u32[]{:S(2)}) collective-permute-start(f32[256,128]{1,0:T(8,128)S(1)} %bitcast.135), channel_id=1, source_target_pairs={{0,4},{1,5},{8,12},{9,13},{16,20},{17,21},{24,28},{25,29},{32,36},... | collective-permute-start | bytes 393224 | tf_op jit(solution)/shard_map/ppermute | solution.py:479
  122.4 1.9 collective-permute-start.13
  125.1 4.5 %all-to-all-start.3 = ((f32[32,16,128]{2,1,0:T(8,128)}), f32[32,16,128]{2,1,0:T(8,128)S(1)}, u32[]{:S(2)}, u32[]{:S(2)}) async-start(f32[32,16,128]{2,1,0:T(8,128)} %broadcast_in_dim.278), calls=%async_computation.3 | async-start | bytes 524288 | tf_op jit(solution)/shard_map/all_to_all | solution.py:477
  129.6 1.6 bitcast_select_fusion
  131.2 6.1 %collective-permute-start.15 = (f32[288,128]{1,0:T(8,128)S(1)}, f32[288,128]{1,0:T(8,128)S(1)}, u32[]{:S(2)}, u32[]{:S(2)}) collective-permute-start(f32[288,128]{1,0:T(8,128)S(1)} %get-tuple-element.213), channel_id=1, source_target_pairs={{0,32},{8,40},{64,96},{72,104},{128,160},{136,168},{192,224},{200,... | collective-permute-start | bytes 442376 | tf_op jit(solution)/shard_map/ppermute | solution.py:437
  137.3 1.3 collective-permute-start.16
  138.7 1.3 collective-permute-start.17
  140.0 1.3 collective-permute-start.14
  141.3 2.6 %collective-permute-start.19 = (f32[2048,128]{1,0:T(8,128)}, f32[2048,128]{1,0:T(8,128)S(1)}, u32[]{:S(2)}, u32[]{:S(2)}) collective-permute-start(f32[2048,128]{1,0:T(8,128)} %all-reduce.16.cloned.1.call-done.own_ref), channel_id=1, source_target_pairs={{0,1},{1,0},{2,3},{3,2},{4,5},{5,4},{6,7},{7,6},{8,9},{9,8},{10,11... | collective-permute-start | bytes 3145736 | tf_op jit(solution)/shard_map/ppermute | solution.py:421
  144.6 4.4 %collective-permute-done.16 = f32[288,128]{1,0:T(8,128)S(1)} collective-permute-done((f32[288,128]{1,0:T(8,128)S(1)}, f32[288,128]{1,0:T(8,128)S(1)}, u32[]{:S(2)}, u32[]{:S(2)}) %collective-permute-start.16) | collective-permute-done | bytes 147488 | tf_op jit(solution)/shard_map/ppermute | solution.py:437
  149.0 2.0 collective-permute-done.17
  151.0 2.4 %away_rest.1 = f32[768,128]{1,0:T(8,128)} custom-call(s32[256]{0:T(256)S(1)} %select_reduce_fusion.1.away_ref, f32[224,128]{1,0:T(8,128)S(1)} %bitcast_select_fusion.1.hs_ref.keep_ref, f32[288,128]{1,0:T(8,128)S(1)} %fusion.26.rest_ref), custom_call_target="tpu_custom_call" | custom-call | bytes 6000000 | tf_op jit(solution)/shard_map/away_rest/pallas_call | solution.py:240
  153.4 10.0 %all-to-all-start.4 = ((f32[32,24,128]{2,1,0:T(8,128)}), f32[32,24,128]{2,1,0:T(8,128)S(1)}, u32[]{:S(2)}, u32[]{:S(2)}) async-start(f32[32,24,128]{2,1,0:T(8,128)} %bitcast.67), calls=%async_computation.4 | async-start | bytes 786432 | tf_op jit(solution)/shard_map/all_to_all | solution.py:487
  163.7 2.7 %collective-permute-start.21 = (f32[32,16,128]{2,1,0:T(8,128)S(1)}, f32[32,16,128]{2,1,0:T(8,128)S(1)}, u32[]{:S(2)}, u32[]{:S(2)}) collective-permute-start(f32[32,16,128]{2,1,0:T(8,128)S(1)} %all-to-all-done.3.refs_0_), channel_id=1, source_target_pairs={{0,6},{2,0},{4,2},{6,4},{1,7},{3,1},{5,3},{7,5},{8,14},{10,8},{12,... | collective-permute-start | bytes 786440 | tf_op jit(solution)/shard_map/ppermute | solution.py:421
  167.4 3.5 %collective-permute-start.18 = (f32[256,128]{1,0:T(8,128)S(1)}, f32[256,128]{1,0:T(8,128)S(1)}, u32[]{:S(2)}, u32[]{:S(2)}) collective-permute-start(f32[256,128]{1,0:T(8,128)S(1)} %add_select_fusion.5.late_ref), channel_id=1, source_target_pairs={{0,1},{1,0},{2,3},{3,2},{4,5},{5,4},{6,7},{7,6},{8,9},{9,8},{10,11... | collective-permute-start | bytes 393224 | tf_op jit(solution)/shard_map/ppermute | solution.py:421
  174.4 6.3 %all-to-all-done.4 = f32[32,24,128]{2,1,0:T(8,128)S(1)} async-done(((f32[32,24,128]{2,1,0:T(8,128)}), f32[32,24,128]{2,1,0:T(8,128)S(1)}, u32[]{:S(2)}, u32[]{:S(2)}) %all-to-all-start.4) | async-done | bytes 393248 | tf_op jit(solution)/shard_map/all_to_all | solution.py:487
  180.8 4.0 %collective-permute-start.23 = (f32[4,32,16,128]{3,2,1,0:T(8,128)S(1)}, f32[4,32,16,128]{3,2,1,0:T(8,128)S(1)}, u32[]{:S(2)}, u32[]{:S(2)}) collective-permute-start(f32[4,32,16,128]{3,2,1,0:T(8,128)S(1)} %join.2.piece_ref), channel_id=1, source_target_pairs={{0,1},{1,0},{2,3},{3,2},{4,5},{5,4},{6,7},{7,6},{8,9},{9,8},{10,11... | collective-permute-start | bytes 3145736 | tf_op jit(solution)/shard_map/ppermute | solution.py:421
  184.8 1.4 and_reduce_fusion.5
  186.2 1.4 and_reduce_fusion.3
  189.6 1.3 and_reduce_fusion.2
  191.6 1.4 and_reduce_fusion
  194.2 3.2 %slice_bitcast_fusion = (f32[512,512]{1,0:T(8,128)}, f32[512,512]{1,0:T(8,128)}) fusion(f32[2,512,512]{2,1,0:T(8,128)} %param.13), kind=kLoop, calls=%fused_computation.89 | loop fusion | bytes 4194304 | tf_op jit(solution)/shard_map/squeeze | solution.py:452
  197.4 2.0 patch_rows.1
  199.5 2.0 copy-done
  201.5 12.5 %factors.1 = (bf16[1024,1024]{1,0:T(8,128)(2,1)}, f32[512,512]{1,0:T(8,128)S(1)}) custom-call(s32[8]{0:T(128)S(1)} %stack.43.info_ref, s32[64]{0:T(128)S(1)} %pad_add_fusion.1.row_ref, s32[64]{0:T(128)S(1)} %pad_add_fusion.2.y_ref, f32[2048,128]{1,0:T(8,128)S(1)} %copy-done.2, f32[2048,128]{1,0:T(8,128)S(1)} %copy-done.4, ...), custom_call_target="tpu_custom_call" | custom-call | bytes 36000000 | tf_op jit(solution)/shard_map/factors/pallas_call | solution.py:363
  215.0 14.6 %update.1 = f32[512,16,128]{2,1,0:T(8,128)} custom-call(s32[8]{0:T(128)} %copy-done.9, f32[512,16,128]{2,1,0:T(8,128)} %bitcast.126, bf16[1024,1024]{1,0:T(8,128)(2,1)} %get-tuple-element.115.m_ref, f32[512,512]{1,0:T(8,128)} %copy-done.1, f32[8,4,4,128,128]{4,3,2,1,0:T(8,128)} %bitcast.146), custom_call_target="tpu_custom_call" | custom-call | bytes 30000000 | tf_op jit(solution)/shard_map/update/pallas_call | solution.py:394
  (118 shorter events, 22.5 us)
Async XLA Ops:
  9.5 4.5 %copy-start.19 = (s32[512]{0:T(512)}, s32[512]{0:T(512)S(1)}, u32[]{:S(2)}) copy-start(s32[512]{0:T(512)S(1)} %get-tuple-element.238) | copy-start | bytes 6148
  9.5 4.5 %copy-start.20 = (s32[512]{0:T(512)}, s32[512]{0:T(512)S(1)}, u32[]{:S(2)}) copy-start(s32[512]{0:T(512)S(1)} %get-tuple-element.237) | copy-start | bytes 6148
  9.5 4.5 %copy-start.21 = (s32[512]{0:T(512)}, s32[512]{0:T(512)S(1)}, u32[]{:S(2)}) copy-start(s32[512]{0:T(512)S(1)} %get-tuple-element.184) | copy-start | bytes 6148
  11.9 2.1 copy-start.22
  12.3 27.8 %copy-start.17 = (s32[512]{0:T(512)}, s32[512]{0:T(512)S(1)}, u32[]{:S(2)}) copy-start(s32[512]{0:T(512)S(1)} %get-tuple-element.141) | copy-start | bytes 6148
  12.7 27.6 %copy-start.18 = (s32[512]{0:T(512)}, s32[512]{0:T(512)S(1)}, u32[]{:S(2)}) copy-start(s32[512]{0:T(512)S(1)} %get-tuple-element.139) | copy-start | bytes 6148
  24.9 18.2 %collective-permute-start = (f32[4,224,128]{2,1,0:T(8,128)}, f32[4,224,128]{2,1,0:T(8,128)}, u32[]{:S(2)}, u32[]{:S(2)}) collective-permute-start(f32[4,224,128]{2,1,0:T(8,128)} %bitcast.36), channel_id=1, source_target_pairs={{0,128},{8,136},{1,129},{9,137},{2,130},{10,138},{3,131},{11,139},... | collective-permute-start | bytes 1376264 | tf_op jit(solution)/shard_map/ppermute | solution.py:429
  30.5 22.8 %collective-permute-start.1 = (f32[4,224,128]{2,1,0:T(8,128)}, f32[4,224,128]{2,1,0:T(8,128)}, u32[]{:S(2)}, u32[]{:S(2)}) collective-permute-start(f32[4,224,128]{2,1,0:T(8,128)} %bitcast.37), channel_id=1, source_target_pairs={{0,64},{8,72},{1,65},{9,73},{2,66},{10,74},{3,67},{11,75},{4,68},{... | collective-permute-start | bytes 1376264 | tf_op jit(solution)/shard_map/ppermute | solution.py:429
  32.6 20.7 %collective-permute-start.2 = (f32[4,224,128]{2,1,0:T(8,128)}, f32[4,224,128]{2,1,0:T(8,128)}, u32[]{:S(2)}, u32[]{:S(2)}) collective-permute-start(f32[4,224,128]{2,1,0:T(8,128)} %bitcast.38), channel_id=1, source_target_pairs={{0,192},{8,200},{1,193},{9,201},{2,194},{10,202},{3,195},{11,203},... | collective-permute-start | bytes 1376264 | tf_op jit(solution)/shard_map/ppermute | solution.py:429
  34.6 31.2 %all-to-all-start = ((f32[32,32,128]{2,1,0:T(8,128)}), f32[32,32,128]{2,1,0:T(8,128)S(1)}, u32[]{:S(2)}, u32[]{:S(2)}) async-start(f32[32,32,128]{2,1,0:T(8,128)} %bitcast.48), calls=%async_computation | async-start | bytes 1048576 | tf_op jit(solution)/shard_map/all_to_all | solution.py:457
  40.0 101.3 %all-reduce.16.cloned.1.call-start = ((), (), s32[]{:S(2)}) async-start(), calls=%async_computation.9 | async-start | bytes 2097152 | tf_op jit(solution)/shard_map/psum | solution.py:462
  54.8 4.0 %copy-start.14 = (f32[4,224,128]{2,1,0:T(8,128)}, f32[4,224,128]{2,1,0:T(8,128)S(1)}, u32[]{:S(2)}) copy-start(f32[4,224,128]{2,1,0:T(8,128)S(1)} %add_select_fusion.4) | copy-start | bytes 1376260
  54.9 4.1 %collective-permute-start.3 = (f32[224,128]{1,0:T(8,128)S(1)}, f32[224,128]{1,0:T(8,128)S(1)}, u32[]{:S(2)}, u32[]{:S(2)}) collective-permute-start(f32[224,128]{1,0:T(8,128)S(1)} %get-tuple-element.216), channel_id=1, source_target_pairs={{0,32},{8,40},{64,96},{72,104},{128,160},{136,168},{192,224},{200,... | collective-permute-start | bytes 344072 | tf_op jit(solution)/shard_map/ppermute | solution.py:437
  56.2 6.8 %collective-permute-start.4 = (f32[224,128]{1,0:T(8,128)S(1)}, f32[224,128]{1,0:T(8,128)S(1)}, u32[]{:S(2)}, u32[]{:S(2)}) collective-permute-start(f32[224,128]{1,0:T(8,128)S(1)} %get-tuple-element.215), channel_id=1, source_target_pairs={{0,16},{8,24},{64,80},{72,88},{128,144},{136,152},{192,208},{200,2... | collective-permute-start | bytes 344072 | tf_op jit(solution)/shard_map/ppermute | solution.py:437
  57.5 5.5 %collective-permute-start.5 = (f32[224,128]{1,0:T(8,128)S(1)}, f32[224,128]{1,0:T(8,128)S(1)}, u32[]{:S(2)}, u32[]{:S(2)}) collective-permute-start(f32[224,128]{1,0:T(8,128)S(1)} %get-tuple-element.214), channel_id=1, source_target_pairs={{0,48},{8,56},{64,112},{72,120},{128,176},{136,184},{192,240},{200... | collective-permute-start | bytes 344072 | tf_op jit(solution)/shard_map/ppermute | solution.py:437
  64.7 150.3 %all-gather.3.cloned.1.call-start = ((), (), s32[]{:S(2)}) async-start(), calls=%async_computation.10 | async-start | bytes 9437184 | tf_op jit(solution)/shard_map/all_gather | solution.py:468
  67.1 13.8 %collective-permute-start.6 = (f32[4,128,128]{2,1,0:T(8,128)S(1)}, f32[4,128,128]{2,1,0:T(8,128)S(1)}, u32[]{:S(2)}, u32[]{:S(2)}) collective-permute-start(f32[4,128,128]{2,1,0:T(8,128)S(1)} %bitcast.131), channel_id=1, source_target_pairs={{0,64},{64,128},{128,192},{192,0},{1,65},{65,129},{129,193},{193,1... | collective-permute-start | bytes 786440 | tf_op jit(solution)/shard_map/ppermute | solution.py:421
  70.1 10.8 %collective-permute-start.7 = (f32[4,128,128]{2,1,0:T(8,128)S(1)}, f32[4,128,128]{2,1,0:T(8,128)S(1)}, u32[]{:S(2)}, u32[]{:S(2)}) collective-permute-start(f32[4,128,128]{2,1,0:T(8,128)S(1)} %bitcast.132), channel_id=1, source_target_pairs={{0,192},{64,0},{128,64},{192,128},{1,193},{65,1},{129,65},{193,129... | collective-permute-start | bytes 786440 | tf_op jit(solution)/shard_map/ppermute | solution.py:421
  70.1 10.8 %collective-permute-start.8 = (f32[4,128,128]{2,1,0:T(8,128)S(1)}, f32[4,128,128]{2,1,0:T(8,128)S(1)}, u32[]{:S(2)}, u32[]{:S(2)}) collective-permute-start(f32[4,128,128]{2,1,0:T(8,128)S(1)} %bitcast.133), channel_id=1, source_target_pairs={{0,128},{64,192},{128,0},{192,64},{1,129},{65,193},{129,1},{193,65... | collective-permute-start | bytes 786440 | tf_op jit(solution)/shard_map/ppermute | solution.py:421
  83.2 35.3 %collective-permute-start.10 = (f32[4,288,128]{2,1,0:T(8,128)}, f32[4,288,128]{2,1,0:T(8,128)}, u32[]{:S(2)}, u32[]{:S(2)}) collective-permute-start(f32[4,288,128]{2,1,0:T(8,128)} %get-tuple-element.203), channel_id=1, source_target_pairs={{0,64},{8,72},{1,65},{9,73},{2,66},{10,74},{3,67},{11,75},{4,68},{... | collective-permute-start | bytes 1769480 | tf_op jit(solution)/shard_map/ppermute | solution.py:429
  88.4 30.2 %collective-permute-start.11 = (f32[4,288,128]{2,1,0:T(8,128)}, f32[4,288,128]{2,1,0:T(8,128)}, u32[]{:S(2)}, u32[]{:S(2)}) collective-permute-start(f32[4,288,128]{2,1,0:T(8,128)} %get-tuple-element.202), channel_id=1, source_target_pairs={{0,192},{8,200},{1,193},{9,201},{2,194},{10,202},{3,195},{11,203},... | collective-permute-start | bytes 1769480 | tf_op jit(solution)/shard_map/ppermute | solution.py:429
  91.7 26.8 %collective-permute-start.9 = (f32[4,288,128]{2,1,0:T(8,128)}, f32[4,288,128]{2,1,0:T(8,128)}, u32[]{:S(2)}, u32[]{:S(2)}) collective-permute-start(f32[4,288,128]{2,1,0:T(8,128)} %get-tuple-element.204), channel_id=1, source_target_pairs={{0,128},{8,136},{1,129},{9,137},{2,130},{10,138},{3,131},{11,139},... | collective-permute-start | bytes 1769480 | tf_op jit(solution)/shard_map/ppermute | solution.py:429
  104.8 13.8 %all-to-all-start.2 = ((f32[32,8,128]{2,1,0:T(8,128)}), f32[32,8,128]{2,1,0:T(8,128)S(1)}, u32[]{:S(2)}, u32[]{:S(2)}) async-start(f32[32,8,128]{2,1,0:T(8,128)} %bitcast.56), calls=%async_computation.2 | async-start | bytes 262144 | tf_op jit(solution)/shard_map/all_to_all | solution.py:470
  118.6 21.4 %collective-permute-start.12 = (f32[256,128]{1,0:T(8,128)S(1)}, f32[256,128]{1,0:T(8,128)}, u32[]{:S(2)}, u32[]{:S(2)}) collective-permute-start(f32[256,128]{1,0:T(8,128)S(1)} %bitcast.135), channel_id=1, source_target_pairs={{0,4},{1,5},{8,12},{9,13},{16,20},{17,21},{24,28},{25,29},{32,36},... | collective-permute-start | bytes 393224 | tf_op jit(solution)/shard_map/ppermute | solution.py:479
  122.4 18.9 %collective-permute-start.13 = (f32[256,128]{1,0:T(8,128)S(1)}, f32[256,128]{1,0:T(8,128)}, u32[]{:S(2)}, u32[]{:S(2)}) collective-permute-start(f32[256,128]{1,0:T(8,128)S(1)} %bitcast.136), channel_id=1, source_target_pairs={{0,2},{1,3},{8,10},{9,11},{16,18},{17,19},{24,26},{25,27},{32,34},... | collective-permute-start | bytes 393224 | tf_op jit(solution)/shard_map/ppermute | solution.py:479
  125.1 25.9 %all-to-all-start.3 = ((f32[32,16,128]{2,1,0:T(8,128)}), f32[32,16,128]{2,1,0:T(8,128)S(1)}, u32[]{:S(2)}, u32[]{:S(2)}) async-start(f32[32,16,128]{2,1,0:T(8,128)} %broadcast_in_dim.278), calls=%async_computation.3 | async-start | bytes 524288 | tf_op jit(solution)/shard_map/all_to_all | solution.py:477
  131.2 13.4 %collective-permute-start.15 = (f32[288,128]{1,0:T(8,128)S(1)}, f32[288,128]{1,0:T(8,128)S(1)}, u32[]{:S(2)}, u32[]{:S(2)}) collective-permute-start(f32[288,128]{1,0:T(8,128)S(1)} %get-tuple-element.213), channel_id=1, source_target_pairs={{0,32},{8,40},{64,96},{72,104},{128,160},{136,168},{192,224},{200,... | collective-permute-start | bytes 442376 | tf_op jit(solution)/shard_map/ppermute | solution.py:437
  137.3 11.6 %collective-permute-start.16 = (f32[288,128]{1,0:T(8,128)S(1)}, f32[288,128]{1,0:T(8,128)S(1)}, u32[]{:S(2)}, u32[]{:S(2)}) collective-permute-start(f32[288,128]{1,0:T(8,128)S(1)} %get-tuple-element.212), channel_id=1, source_target_pairs={{0,16},{8,24},{64,80},{72,88},{128,144},{136,152},{192,208},{200,2... | collective-permute-start | bytes 442376 | tf_op jit(solution)/shard_map/ppermute | solution.py:437
  138.7 12.3 %collective-permute-start.17 = (f32[288,128]{1,0:T(8,128)S(1)}, f32[288,128]{1,0:T(8,128)S(1)}, u32[]{:S(2)}, u32[]{:S(2)}) collective-permute-start(f32[288,128]{1,0:T(8,128)S(1)} %get-tuple-element.211), channel_id=1, source_target_pairs={{0,48},{8,56},{64,112},{72,120},{128,176},{136,184},{192,240},{200... | collective-permute-start | bytes 442376 | tf_op jit(solution)/shard_map/ppermute | solution.py:437
  140.0 4.0 %collective-permute-start.14 = (f32[256,128]{1,0:T(8,128)S(1)}, f32[256,128]{1,0:T(8,128)S(1)}, u32[]{:S(2)}, u32[]{:S(2)}) collective-permute-start(f32[256,128]{1,0:T(8,128)S(1)} %bitcast.137), channel_id=1, source_target_pairs={{0,6},{1,7},{8,14},{9,15},{16,22},{17,23},{24,30},{25,31},{32,38},... | collective-permute-start | bytes 393224 | tf_op jit(solution)/shard_map/ppermute | solution.py:479
  141.3 32.1 %collective-permute-start.19 = (f32[2048,128]{1,0:T(8,128)}, f32[2048,128]{1,0:T(8,128)S(1)}, u32[]{:S(2)}, u32[]{:S(2)}) collective-permute-start(f32[2048,128]{1,0:T(8,128)} %all-reduce.16.cloned.1.call-done.own_ref), channel_id=1, source_target_pairs={{0,1},{1,0},{2,3},{3,2},{4,5},{5,4},{6,7},{7,6},{8,9},{9,8},{10,11... | collective-permute-start | bytes 3145736 | tf_op jit(solution)/shard_map/ppermute | solution.py:421
  143.9 19.5 %copy-start.15 = (f32[256,128]{1,0:T(8,128)}, f32[256,128]{1,0:T(8,128)S(1)}, u32[]{:S(2)}) copy-start(f32[256,128]{1,0:T(8,128)S(1)} %collective-permute-done.14) | copy-start | bytes 393220
  153.4 27.3 %all-to-all-start.4 = ((f32[32,24,128]{2,1,0:T(8,128)}), f32[32,24,128]{2,1,0:T(8,128)S(1)}, u32[]{:S(2)}, u32[]{:S(2)}) async-start(f32[32,24,128]{2,1,0:T(8,128)} %bitcast.67), calls=%async_computation.4 | async-start | bytes 786432 | tf_op jit(solution)/shard_map/all_to_all | solution.py:487
  163.4 9.1 %collective-permute-start.20 = (f32[32,16,128]{2,1,0:T(8,128)S(1)}, f32[32,16,128]{2,1,0:T(8,128)S(1)}, u32[]{:S(2)}, u32[]{:S(2)}) collective-permute-start(f32[32,16,128]{2,1,0:T(8,128)S(1)} %all-to-all-done.3.refs_0_), channel_id=1, source_target_pairs={{0,2},{2,4},{4,6},{6,0},{1,3},{3,5},{5,7},{7,1},{8,10},{10,12},{12... | collective-permute-start | bytes 786440 | tf_op jit(solution)/shard_map/ppermute | solution.py:421
  163.7 8.8 %collective-permute-start.21 = (f32[32,16,128]{2,1,0:T(8,128)S(1)}, f32[32,16,128]{2,1,0:T(8,128)S(1)}, u32[]{:S(2)}, u32[]{:S(2)}) collective-permute-start(f32[32,16,128]{2,1,0:T(8,128)S(1)} %all-to-all-done.3.refs_0_), channel_id=1, source_target_pairs={{0,6},{2,0},{4,2},{6,4},{1,7},{3,1},{5,3},{7,5},{8,14},{10,8},{12,... | collective-permute-start | bytes 786440 | tf_op jit(solution)/shard_map/ppermute | solution.py:421
  166.3 7.1 %collective-permute-start.22 = (f32[32,16,128]{2,1,0:T(8,128)S(1)}, f32[32,16,128]{2,1,0:T(8,128)S(1)}, u32[]{:S(2)}, u32[]{:S(2)}) collective-permute-start(f32[32,16,128]{2,1,0:T(8,128)S(1)} %all-to-all-done.3.refs_0_), channel_id=1, source_target_pairs={{0,4},{2,6},{4,0},{6,2},{1,5},{3,7},{5,1},{7,3},{8,12},{10,14},{12... | collective-permute-start | bytes 786440 | tf_op jit(solution)/shard_map/ppermute | solution.py:421
  167.4 4.4 %collective-permute-start.18 = (f32[256,128]{1,0:T(8,128)S(1)}, f32[256,128]{1,0:T(8,128)S(1)}, u32[]{:S(2)}, u32[]{:S(2)}) collective-permute-start(f32[256,128]{1,0:T(8,128)S(1)} %add_select_fusion.5.late_ref), channel_id=1, source_target_pairs={{0,1},{1,0},{2,3},{3,2},{4,5},{5,4},{6,7},{7,6},{8,9},{9,8},{10,11... | collective-permute-start | bytes 393224 | tf_op jit(solution)/shard_map/ppermute | solution.py:421
  180.8 20.6 %collective-permute-start.23 = (f32[4,32,16,128]{3,2,1,0:T(8,128)S(1)}, f32[4,32,16,128]{3,2,1,0:T(8,128)S(1)}, u32[]{:S(2)}, u32[]{:S(2)}) collective-permute-start(f32[4,32,16,128]{3,2,1,0:T(8,128)S(1)} %join.2.piece_ref), channel_id=1, source_target_pairs={{0,1},{1,0},{2,3},{3,2},{4,5},{5,4},{6,7},{7,6},{8,9},{9,8},{10,11... | collective-permute-start | bytes 3145736 | tf_op jit(solution)/shard_map/ppermute | solution.py:421
  194.2 7.2 %copy-start.9 = (s32[8]{0:T(128)}, s32[8]{0:T(128)S(1)}, u32[]{:S(2)}) copy-start(s32[8]{0:T(128)S(1)} %stack.43.info_ref) | copy-start | bytes 100
  194.2 3.2 %copy-start.10 = (f32[1,1,512,4,1,512]{5,4,3,2,1,0:T(1,128)S(1)}, f32[1,1,512,4,1,512]{5,4,3,2,1,0:T(1,128)}, u32[]{:S(2)}) copy-start(f32[1,1,512,4,1,512]{5,4,3,2,1,0:T(1,128)} %param.11) | copy-start | bytes 12582916
  197.4 4.0 %copy-start.2 = (f32[2048,128]{1,0:T(8,128)S(1)}, f32[2048,128]{1,0:T(8,128)}, u32[]{:S(2)}) copy-start(f32[2048,128]{1,0:T(8,128)} %all-reduce.16.cloned.1.call-done.own_ref) | copy-start | bytes 3145732
  197.4 4.0 %copy-start.4 = (f32[2048,128]{1,0:T(8,128)S(1)}, f32[2048,128]{1,0:T(8,128)}, u32[]{:S(2)}) copy-start(f32[2048,128]{1,0:T(8,128)} %copy-done.3) | copy-start | bytes 3145732
  197.4 4.0 %copy-start.5 = (s32[512,128]{1,0:T(8,128)S(1)}, s32[512,128]{1,0:T(8,128)}, u32[]{:S(2)}) copy-start(s32[512,128]{1,0:T(8,128)} %broadcast_in_dim.270.spot0_ref) | copy-start | bytes 786436
  197.4 4.0 %copy-start.6 = (s32[512,128]{1,0:T(8,128)S(1)}, s32[512,128]{1,0:T(8,128)}, u32[]{:S(2)}) copy-start(s32[512,128]{1,0:T(8,128)} %broadcast_in_dim.271.spot1_ref) | copy-start | bytes 786436
  197.4 4.0 %copy-start.8 = (f32[256,128]{1,0:T(8,128)S(1)}, f32[256,128]{1,0:T(8,128)}, u32[]{:S(2)}) copy-start(f32[256,128]{1,0:T(8,128)} %copy-done.7) | copy-start | bytes 393220
  199.4 2.0 copy-start
  201.4 13.5 %copy-start.16 = (s32[2,512]{1,0:T(2,128)S(1)}, s32[2,512]{1,0:T(2,128)}, u32[]{:S(2)}) copy-start(s32[2,512]{1,0:T(2,128)} %param.12) | copy-start | bytes 12292
  214.0 1.0 copy-start.1
  (2 other events, 1.6 us)
Sparse Core Ops, SparseCore 0:
  64.8 51.0 all-reduce.15
Sparse Core Ops, SparseCore 1:
  82.1 118.6 all-gather.2
where the time goes:
time: 238 us; the launch traced here: 237 us
  starting transfers between devices  81.5 us (34%)
  waiting for transfers between devices  46.6 us (20%)
  Pallas kernels  45.2 us (19%)
  other arithmetic  19.9 us (8%)
  between operations  19.2 us (8%)
  local copies, waits for them, and re-layouts  13.7 us (6%)
  blocking collectives  10.9 us (5%)
    ppermute x6, starting transfers between devices, scatter_y(): lax.ppermute(blocks[b], ROW, [(h, b * Z + h) for h in range(2)])  20.4 us
    ppermute x9, starting transfers between devices, shift(): return lax.ppermute(v, axis, [(i, (i + step) % n) for i in range(n)])  17.9 us
    pallas_call x1, Pallas kernels, update(): pl.pallas_call(update_kernel, out_shape=shaped(NB, SUB, LANES), grid=(8,)...  14.6 us
    ppermute x6, starting transfers between devices, scatter_z(): out.append(lax.ppermute(block[k], ROW, pairs))  12.6 us
    pallas_call x1, Pallas kernels, factors(): call(factor_kernel, 'factors', out, specs, 48, 12, scratch)  12.5 us
    ppermute x6, waiting for transfers between devices, scatter_z(): out.append(lax.ppermute(block[k], ROW, pairs))  11.1 us
    all_to_all x1, blocking collectives, body(): piece = lax.all_to_all(mine[0].reshape(8, 16, LANES), COL, 0, 0)  10.9 us
    ppermute x6, waiting for transfers between devices, scatter_y(): lax.ppermute(blocks[b], ROW, [(h, b * Z + h) for h in range(2)])  10.2 us
  transfers between devices with their start and end apart: 30, of which 10 were waited for; matrix products, arithmetic and copies ran while one was open for 9% of the time, Pallas kernels for 9%

commit v1 on v0

--- a/solution.py
+++ b/solution.py
@@ -485,13 +485,14 @@
     rest = jnp.where(z < 2, rest[0], sum(rest_z))
     away = make_away_rest(away_list, keep, rest)
     recv_rest = lax.all_to_all(away.reshape(32, SLOTS * 3, LANES), ROW, 0, 0)
-    recv_rest, late_swap, swap, *pieces = tie(recv_rest, late_swap, swap, *pieces)
+    late_swap, swap, *pieces = tie(late_swap, swap, *pieces)
     piece = join([piece] + pieces)[0]
     piece_swap = shift(piece, "core", 1)
-    base = patch(to_row, from_y, work, recv_first.reshape(-1, LANES), recv_rest.reshape(-1, LANES))
     m, special = factors(
         info, to_row, from_y, panel, swap, late, late_swap, piece, piece_swap, inv0, inv1, spot0, spot1,
     )
+    m, special, recv_rest = tie(m, special, recv_rest)
+    base = patch(to_row, from_y, work, recv_first.reshape(-1, LANES), recv_rest.reshape(-1, LANES))
     out = update(info, base.reshape(NB, SUB, LANES), m, special, rows)
     out = out.reshape(NB * SUB, LANES)
     out = lax.cond(over, lambda o: general(work, pivots, inverses), lambda o: o, out)

time: 238 us -> 240 us (level)
    all_to_all x1, waiting for transfers between devices: 10.1 us -> 0.51 us  [body(): recv_first = lax.all_to_all(away.reshape(32, SLOTS, LANES), ROW, 0, 0)]
    psum x1, waiting for transfers between devices: 0.02 us -> 7.53 us  [body(): panel = lax.psum(panel, 'x')]
    all_to_all x1, waiting for transfers between devices: 6.33 us -> 0.01 us  [body(): recv_rest = lax.all_to_all(away.reshape(32, SLOTS * 3, LANES), ROW, 0, 0)]
    ppermute x9, waiting for transfers between devices: 8.85 us -> 14.6 us  [shift(): return lax.ppermute(v, axis, [(i, (i + step) % n) for i in range(n)])]
    all_to_all x1, starting transfers between devices: 4.48 us -> 9.53 us  [body(): piece = lax.all_to_all(jnp.broadcast_to(piece, (32, 16, LANES)), ROW, 0, 0)]
    ppermute x9, starting transfers between devices: 17.9 us -> 13.9 us  [shift(): return lax.ppermute(v, axis, [(i, (i + step) % n) for i in range(n)])]
  transfers between devices with their start and end apart: 30 -> 30, of which waited for: 10 -> 11; matrix products, arithmetic and copies ran while one was open for 9% -> 8% of each run, Pallas kernels for 9% -> 10%
where the time goes in v1:
time: 240 us; the launch traced here: 238 us
  starting transfers between devices  83.5 us (35%)
  Pallas kernels  46.8 us (20%)
  waiting for transfers between devices  46.6 us (19%)
  between operations  19.1 us (8%)
  other arithmetic  18.1 us (8%)
  local copies, waits for them, and re-layouts  13.2 us (6%)
  blocking collectives  10.9 us (5%)
    ppermute x6, starting transfers between devices, scatter_y(): lax.ppermute(blocks[b], ROW, [(h, b * Z + h) for h in range(2)])  20.3 us
    pallas_call x1, Pallas kernels, update(): pl.pallas_call(update_kernel, out_shape=shaped(NB, SUB, LANES), grid=(8,)...  14.6 us
    ppermute x9, waiting for transfers between devices, shift(): return lax.ppermute(v, axis, [(i, (i + step) % n) for i in range(n)])  14.6 us
    ppermute x9, starting transfers between devices, shift(): return lax.ppermute(v, axis, [(i, (i + step) % n) for i in range(n)])  13.9 us
    pallas_call x1, Pallas kernels, factors(): call(factor_kernel, 'factors', out, specs, 48, 12, scratch)  13.1 us
    ppermute x6, starting transfers between devices, scatter_z(): out.append(lax.ppermute(block[k], ROW, pairs))  12.6 us
    ppermute x6, waiting for transfers between devices, scatter_z(): out.append(lax.ppermute(block[k], ROW, pairs))  11.8 us
    all_to_all x1, blocking collectives, body(): piece = lax.all_to_all(mine[0].reshape(8, 16, LANES), COL, 0, 0)  10.9 us
  transfers between devices with their start and end apart: 30, of which 11 were waited for; matrix products, arithmetic and copies ran while one was open for 8% of the time, Pallas kernels for 10%

profile of v1, /device:TPU:33, one launch (start us, length us, event | category | flops | bytes accessed | tf_op | source)
XLA Modules:
  0.0 238.2 jit_solution(5669459827857023421)
XLA Ops:
  14.0 8.9 %pack.1 = (f32[3584,128]{1,0:T(8,128)S(1)}, f32[4608,128]{1,0:T(8,128)S(1)}, f32[1024,128]{1,0:T(8,128)S(1)}) custom-call(s32[512]{0:T(512)S(1)} %select_reduce_fusion.home_ref, s32[64]{0:T(128)S(1)} %pad_add_fusion.give_ref, f32[8192,128]{1,0:T(8,128)} %bitcast.143), custom_call_target="tpu_custom_call" | custom-call | bytes 24000000 | tf_op jit(solution)/shard_map/pack/pallas_call | solution.py:195
  22.9 1.3 fusion.73
  24.2 5.6 %collective-permute-start = (f32[4,224,128]{2,1,0:T(8,128)}, f32[4,224,128]{2,1,0:T(8,128)}, u32[]{:S(2)}, u32[]{:S(2)}) collective-permute-start(f32[4,224,128]{2,1,0:T(8,128)} %bitcast.36), channel_id=1, source_target_pairs={{0,128},{8,136},{1,129},{9,137},{2,130},{10,138},{3,131},{11,139},... | collective-permute-start | bytes 1376264 | tf_op jit(solution)/shard_map/ppermute | solution.py:429
  29.8 2.1 collective-permute-start.1
  31.9 2.1 collective-permute-start.2
  33.9 5.4 %all-to-all-start = ((f32[32,32,128]{2,1,0:T(8,128)}), f32[32,32,128]{2,1,0:T(8,128)S(1)}, u32[]{:S(2)}, u32[]{:S(2)}) async-start(f32[32,32,128]{2,1,0:T(8,128)} %bitcast.139), calls=%async_computation | async-start | bytes 1048576 | tf_op jit(solution)/shard_map/all_to_all | solution.py:457
  39.7 2.7 %slice_select_fusion = f32[512,4,128]{2,1,0:T(4,128)} fusion(f32[512,16,128]{2,1,0:T(8,128)} %bitcast.144, pred[]{:T(512)S(6)} %eq.411), kind=kLoop, calls=%fused_computation.88 | loop fusion | flops 262144 | bytes 2097153 | tf_op jit(solution)/shard_map/jit(_where)/select_n | solution.py:448
  42.4 10.2 %collective-permute-done.1 = f32[4,224,128]{2,1,0:T(8,128)} collective-permute-done((f32[4,224,128]{2,1,0:T(8,128)}, f32[4,224,128]{2,1,0:T(8,128)}, u32[]{:S(2)}, u32[]{:S(2)}) %collective-permute-start.1) | collective-permute-done | bytes 458784 | tf_op jit(solution)/shard_map/ppermute | solution.py:429
  52.6 1.5 add_select_fusion.4
  54.2 1.3 collective-permute-start.3
  55.5 1.3 collective-permute-start.4
  56.8 1.3 collective-permute-start.5
  58.2 4.0 %collective-permute-done.4 = f32[224,128]{1,0:T(8,128)S(1)} collective-permute-done((f32[224,128]{1,0:T(8,128)S(1)}, f32[224,128]{1,0:T(8,128)S(1)}, u32[]{:S(2)}, u32[]{:S(2)}) %collective-permute-start.4) | collective-permute-done | bytes 114720 | tf_op jit(solution)/shard_map/ppermute | solution.py:437
  66.3 3.0 %collective-permute-start.6 = (f32[4,128,128]{2,1,0:T(8,128)S(1)}, f32[4,128,128]{2,1,0:T(8,128)S(1)}, u32[]{:S(2)}, u32[]{:S(2)}) collective-permute-start(f32[4,128,128]{2,1,0:T(8,128)S(1)} %bitcast.131), channel_id=1, source_target_pairs={{0,64},{64,128},{128,192},{192,0},{1,65},{65,129},{129,193},{193,1... | collective-permute-start | bytes 786440 | tf_op jit(solution)/shard_map/ppermute | solution.py:421
  69.4 1.9 collective-permute-start.8
  71.4 1.8 away_first.1
  73.2 6.9 %collective-permute-done.6.refs_1_ = f32[4,128,128]{2,1,0:T(8,128)S(1)} collective-permute-done((f32[4,128,128]{2,1,0:T(8,128)S(1)}, f32[4,128,128]{2,1,0:T(8,128)S(1)}, u32[]{:S(2)}, u32[]{:S(2)}) %collective-permute-start.6) | collective-permute-done | bytes 262176 | tf_op jit(solution)/shard_map/ppermute | solution.py:421
  81.2 1.3 slice_bitcast_fusion.2
  82.6 5.1 %collective-permute-start.10 = (f32[4,288,128]{2,1,0:T(8,128)}, f32[4,288,128]{2,1,0:T(8,128)}, u32[]{:S(2)}, u32[]{:S(2)}) collective-permute-start(f32[4,288,128]{2,1,0:T(8,128)} %get-tuple-element.207), channel_id=1, source_target_pairs={{0,64},{8,72},{1,65},{9,73},{2,66},{10,74},{3,67},{11,75},{4,68},{... | collective-permute-start | bytes 1769480 | tf_op jit(solution)/shard_map/ppermute | solution.py:429
  87.7 3.4 %collective-permute-start.11 = (f32[4,288,128]{2,1,0:T(8,128)}, f32[4,288,128]{2,1,0:T(8,128)}, u32[]{:S(2)}, u32[]{:S(2)}) collective-permute-start(f32[4,288,128]{2,1,0:T(8,128)} %get-tuple-element.206), channel_id=1, source_target_pairs={{0,192},{8,200},{1,193},{9,201},{2,194},{10,202},{3,195},{11,203},... | collective-permute-start | bytes 1769480 | tf_op jit(solution)/shard_map/ppermute | solution.py:429
  91.1 2.1 collective-permute-start.9
  93.2 10.9 %all_to_all.25 = f32[8,16,128]{2,1,0:T(8,128)S(1)} all-to-all(f32[8,16,128]{2,1,0:T(8,128)S(1)} %bitcast.151), channel_id=1, replica_groups=mesh['y'=4,'z'=8,'x'=4,'core'=2] {'x','core'}, dimensions={0} | all-to-all | bytes 131072 | tf_op jit(solution)/shard_map/all_to_all | solution.py:472
  104.1 3.6 %all-to-all-start.2 = ((f32[32,8,128]{2,1,0:T(8,128)}), f32[32,8,128]{2,1,0:T(8,128)S(1)}, u32[]{:S(2)}, u32[]{:S(2)}) async-start(f32[32,8,128]{2,1,0:T(8,128)} %bitcast.56), calls=%async_computation.2 | async-start | bytes 262144 | tf_op jit(solution)/shard_map/all_to_all | solution.py:470
  107.7 7.5 %all-reduce.16.cloned.1.call-done.own_ref = f32[2048,128]{1,0:T(8,128)} async-done(((f32[2048,128]{1,0:T(8,128)}), f32[2048,128]{1,0:T(8,128)}) %all-reduce.16.cloned.1.call-update) | async-done | bytes 1048592 | tf_op jit(solution)/shard_map/psum | solution.py:462
  115.2 2.1 collective-permute-start.19
  117.9 4.4 %collective-permute-start.12 = (f32[256,128]{1,0:T(8,128)S(1)}, f32[256,128]{1,0:T(8,128)}, u32[]{:S(2)}, u32[]{:S(2)}) collective-permute-start(f32[256,128]{1,0:T(8,128)S(1)} %bitcast.135), channel_id=1, source_target_pairs={{0,4},{1,5},{8,12},{9,13},{16,20},{17,21},{24,28},{25,29},{32,36},... | collective-permute-start | bytes 393224 | tf_op jit(solution)/shard_map/ppermute | solution.py:479
  122.2 1.9 collective-permute-start.13
  124.9 9.5 %all-to-all-start.3 = ((f32[32,16,128]{2,1,0:T(8,128)}), f32[32,16,128]{2,1,0:T(8,128)S(1)}, u32[]{:S(2)}, u32[]{:S(2)}) async-start(f32[32,16,128]{2,1,0:T(8,128)} %broadcast_in_dim.278), calls=%async_computation.3 | async-start | bytes 524288 | tf_op jit(solution)/shard_map/all_to_all | solution.py:477
  134.4 1.6 bitcast_select_fusion
  136.0 6.1 %collective-permute-start.15 = (f32[288,128]{1,0:T(8,128)S(1)}, f32[288,128]{1,0:T(8,128)S(1)}, u32[]{:S(2)}, u32[]{:S(2)}) collective-permute-start(f32[288,128]{1,0:T(8,128)S(1)} %get-tuple-element.217), channel_id=1, source_target_pairs={{0,32},{8,40},{64,96},{72,104},{128,160},{136,168},{192,224},{200,... | collective-permute-start | bytes 442376 | tf_op jit(solution)/shard_map/ppermute | solution.py:437
  142.2 1.3 collective-permute-start.16
  143.5 1.3 collective-permute-start.17
  144.8 1.3 collective-permute-start.14
  146.1 1.9 collective-permute-done.14
  148.0 1.4 collective-permute-done.15
  149.5 5.1 %collective-permute-done.16 = f32[288,128]{1,0:T(8,128)S(1)} collective-permute-done((f32[288,128]{1,0:T(8,128)S(1)}, f32[288,128]{1,0:T(8,128)S(1)}, u32[]{:S(2)}, u32[]{:S(2)}) %collective-permute-start.16) | collective-permute-done | bytes 147488 | tf_op jit(solution)/shard_map/ppermute | solution.py:437
  155.8 2.7 %collective-permute-start.21 = (f32[32,16,128]{2,1,0:T(8,128)S(1)}, f32[32,16,128]{2,1,0:T(8,128)S(1)}, u32[]{:S(2)}, u32[]{:S(2)}) collective-permute-start(f32[32,16,128]{2,1,0:T(8,128)S(1)} %all-to-all-done.3.refs_0_), channel_id=1, source_target_pairs={{0,6},{2,0},{4,2},{6,4},{1,7},{3,1},{5,3},{7,5},{8,14},{10,8},{12,... | collective-permute-start | bytes 786440 | tf_op jit(solution)/shard_map/ppermute | solution.py:421
  159.5 1.9 collective-permute-start.18
  162.5 6.7 %collective-permute-done.20.refs_1_ = f32[32,16,128]{2,1,0:T(8,128)S(1)} collective-permute-done((f32[32,16,128]{2,1,0:T(8,128)S(1)}, f32[32,16,128]{2,1,0:T(8,128)S(1)}, u32[]{:S(2)}, u32[]{:S(2)}) %collective-permute-start.20) | collective-permute-done | bytes 262176 | tf_op jit(solution)/shard_map/ppermute | solution.py:421
  169.2 2.3 collective-permute-start.23
  172.6 2.4 %away_rest.1 = f32[768,128]{1,0:T(8,128)} custom-call(s32[256]{0:T(256)S(1)} %select_reduce_fusion.1.away_ref, f32[224,128]{1,0:T(8,128)S(1)} %bitcast_select_fusion.1.hs_ref.keep_ref, f32[288,128]{1,0:T(8,128)S(1)} %fusion.26.rest_ref), custom_call_target="tpu_custom_call" | custom-call | bytes 6000000 | tf_op jit(solution)/shard_map/away_rest/pallas_call | solution.py:240
  175.0 10.5 %all-to-all-start.4 = ((f32[32,24,128]{2,1,0:T(8,128)}), f32[32,24,128]{2,1,0:T(8,128)S(1)}, u32[]{:S(2)}, u32[]{:S(2)}) async-start(f32[32,24,128]{2,1,0:T(8,128)} %bitcast.69), calls=%async_computation.4 | async-start | bytes 786432 | tf_op jit(solution)/shard_map/all_to_all | solution.py:487
  192.1 3.0 %slice_bitcast_fusion = (f32[512,512]{1,0:T(8,128)}, f32[512,512]{1,0:T(8,128)}) fusion(f32[2,512,512]{2,1,0:T(8,128)} %param.13), kind=kLoop, calls=%fused_computation.89 | loop fusion | bytes 4194304 | tf_op jit(solution)/shard_map/squeeze | solution.py:452
  195.2 1.2 copy-done.2
  196.4 13.1 %factors.1 = (bf16[1024,1024]{1,0:T(8,128)(2,1)}, f32[512,512]{1,0:T(8,128)S(1)}) custom-call(s32[8]{0:T(128)S(1)} %stack.43.info_ref, s32[64]{0:T(128)S(1)} %pad_add_fusion.1.row_ref, s32[64]{0:T(128)S(1)} %pad_add_fusion.2.y_ref, f32[2048,128]{1,0:T(8,128)S(1)} %copy-done.2, f32[2048,128]{1,0:T(8,128)} %collective-permute-done.19.swap_ref, ...), custom_call_target="tpu_custom_call" | custom-call | bytes 36000000 | tf_op jit(solution)/shard_map/factors/pallas_call | solution.py:363
  210.5 3.7 %patch_rows.1 = f32[8192,128]{1,0:T(8,128)S(1)} custom-call(s32[64]{0:T(128)S(1)} %pad_add_fusion.1.row_ref, s32[64]{0:T(128)S(1)} %pad_add_fusion.2.y_ref, f32[8192,128]{1,0:T(8,128)} %bitcast.145, f32[256,128]{1,0:T(8,128)S(1)} %bitcast.138, f32[768,128]{1,0:T(8,128)S(1)} %bitcast.130), custom_call_target="tpu_custom_call" | custom-call | bytes 12000000 | tf_op jit(solution)/shard_map/patch_rows/pallas_call | solution.py:264
  214.2 2.0 copy-done
  216.2 14.6 %update.1 = f32[512,16,128]{2,1,0:T(8,128)} custom-call(s32[8]{0:T(128)} %copy-done.6, f32[512,16,128]{2,1,0:T(8,128)} %bitcast.126, bf16[1024,1024]{1,0:T(8,128)(2,1)} %get-tuple-element.119.m_ref, f32[512,512]{1,0:T(8,128)} %copy-done.1, f32[8,4,4,128,128]{4,3,2,1,0:T(8,128)} %bitcast.147), custom_call_target="tpu_custom_call" | custom-call | bytes 30000000 | tf_op jit(solution)/shard_map/update/pallas_call | solution.py:394
  (102 shorter events, 21.8 us)
Async XLA Ops:
  22.9 11.1 %copy-start.5 = (f32[1024,128]{1,0:T(8,128)}, f32[1024,128]{1,0:T(8,128)S(1)}, u32[]{:S(2)}) copy-start(f32[1024,128]{1,0:T(8,128)S(1)} %get-tuple-element.92) | copy-start | bytes 1572868
  24.2 18.2 %collective-permute-start = (f32[4,224,128]{2,1,0:T(8,128)}, f32[4,224,128]{2,1,0:T(8,128)}, u32[]{:S(2)}, u32[]{:S(2)}) collective-permute-start(f32[4,224,128]{2,1,0:T(8,128)} %bitcast.36), channel_id=1, source_target_pairs={{0,128},{8,136},{1,129},{9,137},{2,130},{10,138},{3,131},{11,139},... | collective-permute-start | bytes 1376264 | tf_op jit(solution)/shard_map/ppermute | solution.py:429
  29.8 22.8 %collective-permute-start.1 = (f32[4,224,128]{2,1,0:T(8,128)}, f32[4,224,128]{2,1,0:T(8,128)}, u32[]{:S(2)}, u32[]{:S(2)}) collective-permute-start(f32[4,224,128]{2,1,0:T(8,128)} %bitcast.37), channel_id=1, source_target_pairs={{0,64},{8,72},{1,65},{9,73},{2,66},{10,74},{3,67},{11,75},{4,68},{... | collective-permute-start | bytes 1376264 | tf_op jit(solution)/shard_map/ppermute | solution.py:429
  31.9 20.7 %collective-permute-start.2 = (f32[4,224,128]{2,1,0:T(8,128)}, f32[4,224,128]{2,1,0:T(8,128)}, u32[]{:S(2)}, u32[]{:S(2)}) collective-permute-start(f32[4,224,128]{2,1,0:T(8,128)} %bitcast.38), channel_id=1, source_target_pairs={{0,192},{8,200},{1,193},{9,201},{2,194},{10,202},{3,195},{11,203},... | collective-permute-start | bytes 1376264 | tf_op jit(solution)/shard_map/ppermute | solution.py:429
  33.9 31.2 %all-to-all-start = ((f32[32,32,128]{2,1,0:T(8,128)}), f32[32,32,128]{2,1,0:T(8,128)S(1)}, u32[]{:S(2)}, u32[]{:S(2)}) async-start(f32[32,32,128]{2,1,0:T(8,128)} %bitcast.139), calls=%async_computation | async-start | bytes 1048576 | tf_op jit(solution)/shard_map/all_to_all | solution.py:457
  39.3 75.9 %all-reduce.16.cloned.1.call-start = ((), (), s32[]{:S(2)}) async-start(), calls=%async_computation.9 | async-start | bytes 2097152 | tf_op jit(solution)/shard_map/psum | solution.py:462
  54.1 4.0 %copy-start.10 = (f32[4,224,128]{2,1,0:T(8,128)}, f32[4,224,128]{2,1,0:T(8,128)S(1)}, u32[]{:S(2)}) copy-start(f32[4,224,128]{2,1,0:T(8,128)S(1)} %add_select_fusion.4) | copy-start | bytes 1376260
  54.2 4.1 %collective-permute-start.3 = (f32[224,128]{1,0:T(8,128)S(1)}, f32[224,128]{1,0:T(8,128)S(1)}, u32[]{:S(2)}, u32[]{:S(2)}) collective-permute-start(f32[224,128]{1,0:T(8,128)S(1)} %get-tuple-element.220), channel_id=1, source_target_pairs={{0,32},{8,40},{64,96},{72,104},{128,160},{136,168},{192,224},{200,... | collective-permute-start | bytes 344072 | tf_op jit(solution)/shard_map/ppermute | solution.py:437
  55.5 6.8 %collective-permute-start.4 = (f32[224,128]{1,0:T(8,128)S(1)}, f32[224,128]{1,0:T(8,128)S(1)}, u32[]{:S(2)}, u32[]{:S(2)}) collective-permute-start(f32[224,128]{1,0:T(8,128)S(1)} %get-tuple-element.219), channel_id=1, source_target_pairs={{0,16},{8,24},{64,80},{72,88},{128,144},{136,152},{192,208},{200,2... | collective-permute-start | bytes 344072 | tf_op jit(solution)/shard_map/ppermute | solution.py:437
  56.8 5.5 %collective-permute-start.5 = (f32[224,128]{1,0:T(8,128)S(1)}, f32[224,128]{1,0:T(8,128)S(1)}, u32[]{:S(2)}, u32[]{:S(2)}) collective-permute-start(f32[224,128]{1,0:T(8,128)S(1)} %get-tuple-element.218), channel_id=1, source_target_pairs={{0,48},{8,56},{64,112},{72,120},{128,176},{136,184},{192,240},{200... | collective-permute-start | bytes 344072 | tf_op jit(solution)/shard_map/ppermute | solution.py:437
  64.0 152.2 %all-gather.3.cloned.1.call-start = ((), (), s32[]{:S(2)}) async-start(), calls=%async_computation.10 | async-start | bytes 9437184 | tf_op jit(solution)/shard_map/all_gather | solution.py:468
  66.3 13.8 %collective-permute-start.6 = (f32[4,128,128]{2,1,0:T(8,128)S(1)}, f32[4,128,128]{2,1,0:T(8,128)S(1)}, u32[]{:S(2)}, u32[]{:S(2)}) collective-permute-start(f32[4,128,128]{2,1,0:T(8,128)S(1)} %bitcast.131), channel_id=1, source_target_pairs={{0,64},{64,128},{128,192},{192,0},{1,65},{65,129},{129,193},{193,1... | collective-permute-start | bytes 786440 | tf_op jit(solution)/shard_map/ppermute | solution.py:421
  69.4 10.8 %collective-permute-start.7 = (f32[4,128,128]{2,1,0:T(8,128)S(1)}, f32[4,128,128]{2,1,0:T(8,128)S(1)}, u32[]{:S(2)}, u32[]{:S(2)}) collective-permute-start(f32[4,128,128]{2,1,0:T(8,128)S(1)} %bitcast.132), channel_id=1, source_target_pairs={{0,192},{64,0},{128,64},{192,128},{1,193},{65,1},{129,65},{193,129... | collective-permute-start | bytes 786440 | tf_op jit(solution)/shard_map/ppermute | solution.py:421
  69.4 10.8 %collective-permute-start.8 = (f32[4,128,128]{2,1,0:T(8,128)S(1)}, f32[4,128,128]{2,1,0:T(8,128)S(1)}, u32[]{:S(2)}, u32[]{:S(2)}) collective-permute-start(f32[4,128,128]{2,1,0:T(8,128)S(1)} %bitcast.133), channel_id=1, source_target_pairs={{0,128},{64,192},{128,0},{192,64},{1,129},{65,193},{129,1},{193,65... | collective-permute-start | bytes 786440 | tf_op jit(solution)/shard_map/ppermute | solution.py:421
  82.6 35.3 %collective-permute-start.10 = (f32[4,288,128]{2,1,0:T(8,128)}, f32[4,288,128]{2,1,0:T(8,128)}, u32[]{:S(2)}, u32[]{:S(2)}) collective-permute-start(f32[4,288,128]{2,1,0:T(8,128)} %get-tuple-element.207), channel_id=1, source_target_pairs={{0,64},{8,72},{1,65},{9,73},{2,66},{10,74},{3,67},{11,75},{4,68},{... | collective-permute-start | bytes 1769480 | tf_op jit(solution)/shard_map/ppermute | solution.py:429
  87.7 30.2 %collective-permute-start.11 = (f32[4,288,128]{2,1,0:T(8,128)}, f32[4,288,128]{2,1,0:T(8,128)}, u32[]{:S(2)}, u32[]{:S(2)}) collective-permute-start(f32[4,288,128]{2,1,0:T(8,128)} %get-tuple-element.206), channel_id=1, source_target_pairs={{0,192},{8,200},{1,193},{9,201},{2,194},{10,202},{3,195},{11,203},... | collective-permute-start | bytes 1769480 | tf_op jit(solution)/shard_map/ppermute | solution.py:429
  91.1 26.8 %collective-permute-start.9 = (f32[4,288,128]{2,1,0:T(8,128)}, f32[4,288,128]{2,1,0:T(8,128)}, u32[]{:S(2)}, u32[]{:S(2)}) collective-permute-start(f32[4,288,128]{2,1,0:T(8,128)} %get-tuple-element.208), channel_id=1, source_target_pairs={{0,128},{8,136},{1,129},{9,137},{2,130},{10,138},{3,131},{11,139},... | collective-permute-start | bytes 1769480 | tf_op jit(solution)/shard_map/ppermute | solution.py:429
  104.1 13.8 %all-to-all-start.2 = ((f32[32,8,128]{2,1,0:T(8,128)}), f32[32,8,128]{2,1,0:T(8,128)S(1)}, u32[]{:S(2)}, u32[]{:S(2)}) async-start(f32[32,8,128]{2,1,0:T(8,128)} %bitcast.56), calls=%async_computation.2 | async-start | bytes 262144 | tf_op jit(solution)/shard_map/all_to_all | solution.py:470
  115.2 53.9 %collective-permute-start.19 = (f32[2048,128]{1,0:T(8,128)}, f32[2048,128]{1,0:T(8,128)}, u32[]{:S(2)}, u32[]{:S(2)}) collective-permute-start(f32[2048,128]{1,0:T(8,128)} %all-reduce.16.cloned.1.call-done.own_ref), channel_id=1, source_target_pairs={{0,1},{1,0},{2,3},{3,2},{4,5},{5,4},{6,7},{7,6},{8,9},{9,8},{10,11... | collective-permute-start | bytes 3145736 | tf_op jit(solution)/shard_map/ppermute | solution.py:421
  117.9 25.6 %collective-permute-start.12 = (f32[256,128]{1,0:T(8,128)S(1)}, f32[256,128]{1,0:T(8,128)}, u32[]{:S(2)}, u32[]{:S(2)}) collective-permute-start(f32[256,128]{1,0:T(8,128)S(1)} %bitcast.135), channel_id=1, source_target_pairs={{0,4},{1,5},{8,12},{9,13},{16,20},{17,21},{24,28},{25,29},{32,36},... | collective-permute-start | bytes 393224 | tf_op jit(solution)/shard_map/ppermute | solution.py:479
  122.2 22.6 %collective-permute-start.13 = (f32[256,128]{1,0:T(8,128)S(1)}, f32[256,128]{1,0:T(8,128)}, u32[]{:S(2)}, u32[]{:S(2)}) collective-permute-start(f32[256,128]{1,0:T(8,128)S(1)} %bitcast.136), channel_id=1, source_target_pairs={{0,2},{1,3},{8,10},{9,11},{16,18},{17,19},{24,26},{25,27},{32,34},... | collective-permute-start | bytes 393224 | tf_op jit(solution)/shard_map/ppermute | solution.py:479
  124.9 30.9 %all-to-all-start.3 = ((f32[32,16,128]{2,1,0:T(8,128)}), f32[32,16,128]{2,1,0:T(8,128)S(1)}, u32[]{:S(2)}, u32[]{:S(2)}) async-start(f32[32,16,128]{2,1,0:T(8,128)} %broadcast_in_dim.278), calls=%async_computation.3 | async-start | bytes 524288 | tf_op jit(solution)/shard_map/all_to_all | solution.py:477
  136.0 13.4 %collective-permute-start.15 = (f32[288,128]{1,0:T(8,128)S(1)}, f32[288,128]{1,0:T(8,128)S(1)}, u32[]{:S(2)}, u32[]{:S(2)}) collective-permute-start(f32[288,128]{1,0:T(8,128)S(1)} %get-tuple-element.217), channel_id=1, source_target_pairs={{0,32},{8,40},{64,96},{72,104},{128,160},{136,168},{192,224},{200,... | collective-permute-start | bytes 442376 | tf_op jit(solution)/shard_map/ppermute | solution.py:437
  142.2 12.4 %collective-permute-start.16 = (f32[288,128]{1,0:T(8,128)S(1)}, f32[288,128]{1,0:T(8,128)S(1)}, u32[]{:S(2)}, u32[]{:S(2)}) collective-permute-start(f32[288,128]{1,0:T(8,128)S(1)} %get-tuple-element.216), channel_id=1, source_target_pairs={{0,16},{8,24},{64,80},{72,88},{128,144},{136,152},{192,208},{200,2... | collective-permute-start | bytes 442376 | tf_op jit(solution)/shard_map/ppermute | solution.py:437
  143.5 12.3 %collective-permute-start.17 = (f32[288,128]{1,0:T(8,128)S(1)}, f32[288,128]{1,0:T(8,128)S(1)}, u32[]{:S(2)}, u32[]{:S(2)}) collective-permute-start(f32[288,128]{1,0:T(8,128)S(1)} %get-tuple-element.215), channel_id=1, source_target_pairs={{0,48},{8,56},{64,112},{72,120},{128,176},{136,184},{192,240},{200... | collective-permute-start | bytes 442376 | tf_op jit(solution)/shard_map/ppermute | solution.py:437
  144.8 3.2 %collective-permute-start.14 = (f32[256,128]{1,0:T(8,128)S(1)}, f32[256,128]{1,0:T(8,128)S(1)}, u32[]{:S(2)}, u32[]{:S(2)}) collective-permute-start(f32[256,128]{1,0:T(8,128)S(1)} %bitcast.137), channel_id=1, source_target_pairs={{0,6},{1,7},{8,14},{9,15},{16,22},{17,23},{24,30},{25,31},{32,38},... | collective-permute-start | bytes 393224 | tf_op jit(solution)/shard_map/ppermute | solution.py:479
  149.5 9.0 %copy-start.11 = (f32[288,128]{1,0:T(8,128)}, f32[288,128]{1,0:T(8,128)S(1)}, u32[]{:S(2)}) copy-start(f32[288,128]{1,0:T(8,128)S(1)} %collective-permute-done.15) | copy-start | bytes 442372
  154.6 3.9 %copy-start.12 = (f32[288,128]{1,0:T(8,128)}, f32[288,128]{1,0:T(8,128)S(1)}, u32[]{:S(2)}) copy-start(f32[288,128]{1,0:T(8,128)S(1)} %collective-permute-done.16) | copy-start | bytes 442372
  155.8 2.7 %copy-start.13 = (f32[288,128]{1,0:T(8,128)}, f32[288,128]{1,0:T(8,128)S(1)}, u32[]{:S(2)}) copy-start(f32[288,128]{1,0:T(8,128)S(1)} %collective-permute-done.17) | copy-start | bytes 442372
  155.8 13.3 %collective-permute-start.20 = (f32[32,16,128]{2,1,0:T(8,128)S(1)}, f32[32,16,128]{2,1,0:T(8,128)S(1)}, u32[]{:S(2)}, u32[]{:S(2)}) collective-permute-start(f32[32,16,128]{2,1,0:T(8,128)S(1)} %all-to-all-done.3.refs_0_), channel_id=1, source_target_pairs={{0,2},{2,4},{4,6},{6,0},{1,3},{3,5},{5,7},{7,1},{8,10},{10,12},{12... | collective-permute-start | bytes 786440 | tf_op jit(solution)/shard_map/ppermute | solution.py:421
  155.8 13.3 %collective-permute-start.21 = (f32[32,16,128]{2,1,0:T(8,128)S(1)}, f32[32,16,128]{2,1,0:T(8,128)S(1)}, u32[]{:S(2)}, u32[]{:S(2)}) collective-permute-start(f32[32,16,128]{2,1,0:T(8,128)S(1)} %all-to-all-done.3.refs_0_), channel_id=1, source_target_pairs={{0,6},{2,0},{4,2},{6,4},{1,7},{3,1},{5,3},{7,5},{8,14},{10,8},{12,... | collective-permute-start | bytes 786440 | tf_op jit(solution)/shard_map/ppermute | solution.py:421
  158.5 10.7 %collective-permute-start.22 = (f32[32,16,128]{2,1,0:T(8,128)S(1)}, f32[32,16,128]{2,1,0:T(8,128)S(1)}, u32[]{:S(2)}, u32[]{:S(2)}) collective-permute-start(f32[32,16,128]{2,1,0:T(8,128)S(1)} %all-to-all-done.3.refs_0_), channel_id=1, source_target_pairs={{0,4},{2,6},{4,0},{6,2},{1,5},{3,7},{5,1},{7,3},{8,12},{10,14},{12... | collective-permute-start | bytes 786440 | tf_op jit(solution)/shard_map/ppermute | solution.py:421
  159.5 35.7 %copy-start.3 = (s32[512,128]{1,0:T(8,128)S(1)}, s32[512,128]{1,0:T(8,128)}, u32[]{:S(2)}) copy-start(s32[512,128]{1,0:T(8,128)} %broadcast_in_dim.270.spot0_ref) | copy-start | bytes 786436
  159.5 35.6 %copy-start.4 = (s32[512,128]{1,0:T(8,128)S(1)}, s32[512,128]{1,0:T(8,128)}, u32[]{:S(2)}) copy-start(s32[512,128]{1,0:T(8,128)} %broadcast_in_dim.271.spot1_ref) | copy-start | bytes 786436
  159.5 2.9 %collective-permute-start.18 = (f32[256,128]{1,0:T(8,128)S(1)}, f32[256,128]{1,0:T(8,128)S(1)}, u32[]{:S(2)}, u32[]{:S(2)}) collective-permute-start(f32[256,128]{1,0:T(8,128)S(1)} %add_select_fusion.5.late_ref), channel_id=1, source_target_pairs={{0,1},{1,0},{2,3},{3,2},{4,5},{5,4},{6,7},{7,6},{8,9},{9,8},{10,11... | collective-permute-start | bytes 393224 | tf_op jit(solution)/shard_map/ppermute | solution.py:421
  169.2 26.0 %collective-permute-start.23 = (f32[4,32,16,128]{3,2,1,0:T(8,128)S(1)}, f32[4,32,16,128]{3,2,1,0:T(8,128)}, u32[]{:S(2)}, u32[]{:S(2)}) collective-permute-start(f32[4,32,16,128]{3,2,1,0:T(8,128)S(1)} %join.2.piece_ref), channel_id=1, source_target_pairs={{0,1},{1,0},{2,3},{3,2},{4,5},{5,4},{6,7},{7,6},{8,9},{9,8},{10,11... | collective-permute-start | bytes 3145736 | tf_op jit(solution)/shard_map/ppermute | solution.py:421
  175.0 35.5 %all-to-all-start.4 = ((f32[32,24,128]{2,1,0:T(8,128)}), f32[32,24,128]{2,1,0:T(8,128)S(1)}, u32[]{:S(2)}, u32[]{:S(2)}) async-start(f32[32,24,128]{2,1,0:T(8,128)} %bitcast.69), calls=%async_computation.4 | async-start | bytes 786432 | tf_op jit(solution)/shard_map/all_to_all | solution.py:487
  192.1 17.4 %copy-start.6 = (s32[8]{0:T(128)}, s32[8]{0:T(128)S(1)}, u32[]{:S(2)}) copy-start(s32[8]{0:T(128)S(1)} %stack.43.info_ref) | copy-start | bytes 100
  195.2 1.2 copy-start.2
  209.5 1.0 copy-start.1
  210.5 5.6 %copy-start.14 = (s32[2,512]{1,0:T(2,128)S(1)}, s32[2,512]{1,0:T(2,128)}, u32[]{:S(2)}) copy-start(s32[2,512]{1,0:T(2,128)} %param.12) | copy-start | bytes 12292
  214.2 2.0 copy-start
Sparse Core Ops, SparseCore 0:
  64.1 51.1 all-reduce.15
Sparse Core Ops, SparseCore 1:
  81.3 118.6 all-gather.2

commit v2 on v0

--- a/solution.py
+++ b/solution.py
@@ -279,7 +279,7 @@
 
 def factor_kernel(
     info_ref, row_ref, y_ref, own_ref, swap_ref, late_ref, late_swap, piece_ref, piece_swap,
-    inv0_ref, inv1_ref, spot0_ref, spot1_ref,
+    inv_ref, spot0_ref, spot1_ref,
     m_ref, sp_ref, a0, a1, u01, p0, lin0, lin1,
 ):
     r, c, x, core = info_ref[4], info_ref[5], info_ref[6], info_ref[7]
@@ -320,7 +320,7 @@
     place = lax.broadcasted_iota(I32, (NB, NB), 1)
     hot0 = jnp.where(spot0_ref[:, :1] == place, 1.0, 0.0)
     hot1 = jnp.where(spot1_ref[:, :1] == place, 1.0, 0.0)
-    inv0, inv1 = split(inv0_ref[...]), split(inv1_ref[...])
+    inv0, inv1 = split(inv_ref[0]), split(inv_ref[1])
 
     def turned(inv, hot):
         hot = hot.astype(jnp.bfloat16)
@@ -449,7 +449,6 @@
     home_list, give_list, slice_list, away_list, to_row, from_y, hot, over = plan(pivots, y, z)
     is_special = ((c == 0) & (r >= 1)) | ((c == 1) & (r >= 2))
     info = jnp.stack([y, z, (r < 2).astype(I32), is_special.astype(I32), r, c, x, core])
-    inv0, inv1 = inverses[0], inverses[1]
 
     keep, rest, send = pack(home_list, give_list, work)
     keep, rest = keep.reshape(4, 4, WAVE, LANES), rest.reshape(4, 4, REST * 3, LANES)
@@ -457,7 +456,7 @@
     recv = lax.all_to_all(send.reshape(32, 4 * SLOTS, LANES), ROW, 0, 0)
     keep = jnp.where(y == 0, keep[0], sum(keep_y))
     keep_z = scatter_z(keep)
-    keep, panel, to_row, from_y, spot0, spot1, *keep_z = tie(keep, panel, to_row, from_y, *hot, *keep_z)
+    keep, panel, spot0, spot1, *keep_z = tie(keep, panel, *hot, *keep_z)
     keep = jnp.where(z < 2, keep[0], sum(keep_z))
     panel = lax.psum(panel, "x")
     mine = make_slice(slice_list, keep, recv.reshape(-1, LANES)).reshape(4, 128, LANES)
@@ -470,7 +469,8 @@
     recv_first = lax.all_to_all(away.reshape(32, SLOTS, LANES), ROW, 0, 0)
     rest_y = scatter_y(rest)
     piece = lax.all_to_all(mine[0].reshape(8, 16, LANES), COL, 0, 0)
-    piece, recv_first, *rest_y = tie(piece, recv_first, *rest_y)
+    over = over.astype(I32)
+    piece, recv_first, over, to_row, from_y, *rest_y = tie(piece, recv_first, over, to_row, from_y, *rest_y)
     rest = jnp.where(y == 0, rest[0], sum(rest_y))
     rest_z = scatter_z(rest)
     piece = lax.dynamic_slice_in_dim(piece, 1 - z % 2, 1, 0)
@@ -490,11 +490,11 @@
     piece_swap = shift(piece, "core", 1)
     base = patch(to_row, from_y, work, recv_first.reshape(-1, LANES), recv_rest.reshape(-1, LANES))
     m, special = factors(
-        info, to_row, from_y, panel, swap, late, late_swap, piece, piece_swap, inv0, inv1, spot0, spot1,
+        info, to_row, from_y, panel, swap, late, late_swap, piece, piece_swap, inverses, spot0, spot1,
     )
     out = update(info, base.reshape(NB, SUB, LANES), m, special, rows)
     out = out.reshape(NB * SUB, LANES)
-    out = lax.cond(over, lambda o: general(work, pivots, inverses), lambda o: o, out)
+    out = lax.cond(over > 0, lambda o: general(work, pivots, inverses), lambda o: o, out)
     return out.reshape(matrix.shape)
 
 

time: 238 us -> 230 us (0.966)
  blocking collectives: 10.9 us -> 0 us
  starting transfers between devices: 81.5 us -> 87.7 us
    all_to_all x1 -> x0, blocking collectives: 10.9 us -> none  [body(): piece = lax.all_to_all(mine[0].reshape(8, 16, LANES), COL, 0, 0)]
    all_to_all x0 -> x1, starting transfers between devices: none -> 6.24 us  [body(): piece = lax.all_to_all(mine[0].reshape(8, 16, LANES), COL, 0, 0)]
    all_to_all x1, waiting for transfers between devices: 10.1 us -> 4.91 us  [body(): recv_first = lax.all_to_all(away.reshape(32, SLOTS, LANES), ROW, 0, 0)]
    all_to_all x0 -> x1, waiting for transfers between devices: none -> 4.35 us  [body(): piece = lax.all_to_all(mine[0].reshape(8, 16, LANES), COL, 0, 0)]
    squeeze x1 -> x0, local copies, waits for them, and re-layouts: 3.18 us -> none  [body(): inv0, inv1 = (inverses[0], inverses[1])]
    unnamed x40 -> x30, local copies, waits for them, and re-layouts: 4.64 us -> 5.39 us
  transfers between devices with their start and end apart: 30 -> 31, of which waited for: 10 -> 12; matrix products, arithmetic and copies ran while one was open for 9% -> 7% of each run, Pallas kernels for 9% -> 10%
where the time goes in v2:
time: 230 us; the launch traced here: 229 us
  starting transfers between devices  87.7 us (38%)
  waiting for transfers between devices  46.2 us (20%)
  Pallas kernels  46.1 us (20%)
  between operations  19.2 us (8%)
  other arithmetic  17.9 us (8%)
  local copies, waits for them, and re-layouts  11.7 us (5%)
    ppermute x6, starting transfers between devices, scatter_y(): lax.ppermute(blocks[b], ROW, [(h, b * Z + h) for h in range(2)])  20.4 us
    ppermute x9, starting transfers between devices, shift(): return lax.ppermute(v, axis, [(i, (i + step) % n) for i in range(n)])  18.1 us
    pallas_call x1, Pallas kernels, update(): pl.pallas_call(update_kernel, out_shape=shaped(NB, SUB, LANES), grid=(8,)...  14.6 us
    ppermute x6, starting transfers between devices, scatter_z(): out.append(lax.ppermute(block[k], ROW, pairs))  12.6 us
    pallas_call x1, Pallas kernels, factors(): call(factor_kernel, 'factors', out, specs, 48, 12, scratch)  11.5 us
    ppermute x6, waiting for transfers between devices, scatter_z(): out.append(lax.ppermute(block[k], ROW, pairs))  11.1 us
    ppermute x6, waiting for transfers between devices, scatter_y(): lax.ppermute(blocks[b], ROW, [(h, b * Z + h) for h in range(2)])  10.5 us
    all_to_all x1, starting transfers between devices, body(): recv_rest = lax.all_to_all(away.reshape(32, SLOTS * 3, LANES), ROW, 0, 0)  10 us
  transfers between devices with their start and end apart: 31, of which 12 were waited for; matrix products, arithmetic and copies ran while one was open for 7% of the time, Pallas kernels for 10%

profile of v2, /device:TPU:33, one launch (start us, length us, event | category | flops | bytes accessed | tf_op | source)
XLA Modules:
  0.0 228.8 jit_solution(18404688574082465895)
XLA Ops:
  14.0 9.6 %pack.1 = (f32[3584,128]{1,0:T(8,128)S(1)}, f32[4608,128]{1,0:T(8,128)S(1)}, f32[1024,128]{1,0:T(8,128)}) custom-call(s32[512]{0:T(512)S(1)} %select_reduce_fusion.home_ref, s32[64]{0:T(128)S(1)} %pad_add_fusion.give_ref, f32[8192,128]{1,0:T(8,128)} %bitcast.138), custom_call_target="tpu_custom_call" | custom-call | bytes 24000000 | tf_op jit(solution)/shard_map/pack/pallas_call | solution.py:195
  23.6 1.1 fusion.73
  24.7 5.6 %collective-permute-start = (f32[4,224,128]{2,1,0:T(8,128)}, f32[4,224,128]{2,1,0:T(8,128)}, u32[]{:S(2)}, u32[]{:S(2)}) collective-permute-start(f32[4,224,128]{2,1,0:T(8,128)} %bitcast.29), channel_id=1, source_target_pairs={{0,128},{8,136},{1,129},{9,137},{2,130},{10,138},{3,131},{11,139},... | collective-permute-start | bytes 1376264 | tf_op jit(solution)/shard_map/ppermute | solution.py:429
  30.3 2.1 collective-permute-start.1
  32.4 2.1 collective-permute-start.2
  34.5 5.4 %all-to-all-start = ((f32[32,32,128]{2,1,0:T(8,128)}), f32[32,32,128]{2,1,0:T(8,128)S(1)}, u32[]{:S(2)}, u32[]{:S(2)}) async-start(f32[32,32,128]{2,1,0:T(8,128)} %bitcast.38), calls=%async_computation | async-start | bytes 1048576 | tf_op jit(solution)/shard_map/all_to_all | solution.py:456
  39.9 2.7 %slice_select_fusion = f32[512,4,128]{2,1,0:T(4,128)} fusion(f32[512,16,128]{2,1,0:T(8,128)} %bitcast.139, pred[]{:T(512)S(6)} %eq.415), kind=kLoop, calls=%fused_computation.88 | loop fusion | flops 262144 | bytes 2097153 | tf_op jit(solution)/shard_map/jit(_where)/select_n | solution.py:448
  42.7 10.4 %collective-permute-done.1 = f32[4,224,128]{2,1,0:T(8,128)} collective-permute-done((f32[4,224,128]{2,1,0:T(8,128)}, f32[4,224,128]{2,1,0:T(8,128)}, u32[]{:S(2)}, u32[]{:S(2)}) %collective-permute-start.1) | collective-permute-done | bytes 458784 | tf_op jit(solution)/shard_map/ppermute | solution.py:429
  53.1 1.4 add_select_fusion.4
  55.3 1.3 collective-permute-start.3
  56.6 1.3 collective-permute-start.4
  57.9 1.3 collective-permute-start.5
  59.3 4.1 %collective-permute-done.4 = f32[224,128]{1,0:T(8,128)S(1)} collective-permute-done((f32[224,128]{1,0:T(8,128)S(1)}, f32[224,128]{1,0:T(8,128)S(1)}, u32[]{:S(2)}, u32[]{:S(2)}) %collective-permute-start.4) | collective-permute-done | bytes 114720 | tf_op jit(solution)/shard_map/ppermute | solution.py:437
  66.3 1.2 pivot_slice.1
  67.5 3.2 %collective-permute-start.6 = (f32[4,128,128]{2,1,0:T(8,128)S(1)}, f32[4,128,128]{2,1,0:T(8,128)S(1)}, u32[]{:S(2)}, u32[]{:S(2)}) collective-permute-start(f32[4,128,128]{2,1,0:T(8,128)S(1)} %bitcast.127), channel_id=1, source_target_pairs={{0,64},{64,128},{128,192},{192,0},{1,65},{65,129},{129,193},{193,1... | collective-permute-start | bytes 786440 | tf_op jit(solution)/shard_map/ppermute | solution.py:421
  70.7 1.9 collective-permute-start.8
  72.7 1.8 away_first.1
  74.5 6.7 %collective-permute-done.6.refs_1_ = f32[4,128,128]{2,1,0:T(8,128)S(1)} collective-permute-done((f32[4,128,128]{2,1,0:T(8,128)S(1)}, f32[4,128,128]{2,1,0:T(8,128)S(1)}, u32[]{:S(2)}, u32[]{:S(2)}) %collective-permute-start.6) | collective-permute-done | bytes 262176 | tf_op jit(solution)/shard_map/ppermute | solution.py:421
  81.5 1.0 join.3
  82.8 1.3 slice_bitcast_fusion
  84.1 5.2 %collective-permute-start.10 = (f32[4,288,128]{2,1,0:T(8,128)}, f32[4,288,128]{2,1,0:T(8,128)}, u32[]{:S(2)}, u32[]{:S(2)}) collective-permute-start(f32[4,288,128]{2,1,0:T(8,128)} %get-tuple-element.205), channel_id=1, source_target_pairs={{0,64},{8,72},{1,65},{9,73},{2,66},{10,74},{3,67},{11,75},{4,68},{... | collective-permute-start | bytes 1769480 | tf_op jit(solution)/shard_map/ppermute | solution.py:429
  89.2 3.3 %collective-permute-start.11 = (f32[4,288,128]{2,1,0:T(8,128)}, f32[4,288,128]{2,1,0:T(8,128)}, u32[]{:S(2)}, u32[]{:S(2)}) collective-permute-start(f32[4,288,128]{2,1,0:T(8,128)} %get-tuple-element.204), channel_id=1, source_target_pairs={{0,192},{8,200},{1,193},{9,201},{2,194},{10,202},{3,195},{11,203},... | collective-permute-start | bytes 1769480 | tf_op jit(solution)/shard_map/ppermute | solution.py:429
  92.6 2.2 collective-permute-start.9
  96.8 6.2 %all-to-all-start.1 = ((f32[8,16,128]{2,1,0:T(8,128)}), f32[8,16,128]{2,1,0:T(8,128)S(1)}, u32[]{:S(2)}, u32[]{:S(2)}) async-start(f32[8,16,128]{2,1,0:T(8,128)} %bitcast.40), calls=%async_computation.1 | async-start | bytes 131072 | tf_op jit(solution)/shard_map/all_to_all | solution.py:471
  103.7 4.3 %all-to-all-done.1 = f32[8,16,128]{2,1,0:T(8,128)S(1)} async-done(((f32[8,16,128]{2,1,0:T(8,128)}), f32[8,16,128]{2,1,0:T(8,128)S(1)}, u32[]{:S(2)}, u32[]{:S(2)}) %all-to-all-start.1) | async-done | bytes 65568 | tf_op jit(solution)/shard_map/all_to_all | solution.py:471
  108.0 3.6 %all-to-all-start.2 = ((f32[32,8,128]{2,1,0:T(8,128)}), f32[32,8,128]{2,1,0:T(8,128)S(1)}, u32[]{:S(2)}, u32[]{:S(2)}) async-start(f32[32,8,128]{2,1,0:T(8,128)} %bitcast.46), calls=%async_computation.2 | async-start | bytes 262144 | tf_op jit(solution)/shard_map/all_to_all | solution.py:469
  116.4 4.9 %all-to-all-done.2 = f32[32,8,128]{2,1,0:T(8,128)S(1)} async-done(((f32[32,8,128]{2,1,0:T(8,128)}), f32[32,8,128]{2,1,0:T(8,128)S(1)}, u32[]{:S(2)}, u32[]{:S(2)}) %all-to-all-start.2) | async-done | bytes 131104 | tf_op jit(solution)/shard_map/all_to_all | solution.py:469
  121.3 3.6 %collective-permute-start.12 = (f32[256,128]{1,0:T(8,128)S(1)}, f32[256,128]{1,0:T(8,128)S(1)}, u32[]{:S(2)}, u32[]{:S(2)}) collective-permute-start(f32[256,128]{1,0:T(8,128)S(1)} %bitcast.131), channel_id=1, source_target_pairs={{0,4},{1,5},{8,12},{9,13},{16,20},{17,21},{24,28},{25,29},{32,36},... | collective-permute-start | bytes 393224 | tf_op jit(solution)/shard_map/ppermute | solution.py:479
  124.9 1.9 collective-permute-start.13
  127.5 4.5 %all-to-all-start.3 = ((f32[32,16,128]{2,1,0:T(8,128)}), f32[32,16,128]{2,1,0:T(8,128)S(1)}, u32[]{:S(2)}, u32[]{:S(2)}) async-start(f32[32,16,128]{2,1,0:T(8,128)} %broadcast_in_dim.281), calls=%async_computation.3 | async-start | bytes 524288 | tf_op jit(solution)/shard_map/all_to_all | solution.py:477
  132.0 1.5 bitcast_select_fusion
  133.6 6.1 %collective-permute-start.15 = (f32[288,128]{1,0:T(8,128)S(1)}, f32[288,128]{1,0:T(8,128)S(1)}, u32[]{:S(2)}, u32[]{:S(2)}) collective-permute-start(f32[288,128]{1,0:T(8,128)S(1)} %get-tuple-element.213), channel_id=1, source_target_pairs={{0,32},{8,40},{64,96},{72,104},{128,160},{136,168},{192,224},{200,... | collective-permute-start | bytes 442376 | tf_op jit(solution)/shard_map/ppermute | solution.py:437
  139.7 1.3 collective-permute-start.16
  141.0 1.3 collective-permute-start.17
  142.3 1.3 collective-permute-start.14
  143.7 2.7 %collective-permute-start.19 = (f32[2048,128]{1,0:T(8,128)}, f32[2048,128]{1,0:T(8,128)S(1)}, u32[]{:S(2)}, u32[]{:S(2)}) collective-permute-start(f32[2048,128]{1,0:T(8,128)} %all-reduce.16.cloned.1.call-done.own_ref), channel_id=1, source_target_pairs={{0,1},{1,0},{2,3},{3,2},{4,5},{5,4},{6,7},{7,6},{8,9},{9,8},{10,11... | collective-permute-start | bytes 3145736 | tf_op jit(solution)/shard_map/ppermute | solution.py:421
  147.0 4.3 %collective-permute-done.16 = f32[288,128]{1,0:T(8,128)S(1)} collective-permute-done((f32[288,128]{1,0:T(8,128)S(1)}, f32[288,128]{1,0:T(8,128)S(1)}, u32[]{:S(2)}, u32[]{:S(2)}) %collective-permute-start.16) | collective-permute-done | bytes 147488 | tf_op jit(solution)/shard_map/ppermute | solution.py:437
  151.3 2.0 collective-permute-done.17
  154.3 2.4 %away_rest.1 = f32[768,128]{1,0:T(8,128)} custom-call(s32[256]{0:T(256)S(1)} %select_reduce_fusion.1.away_ref, f32[224,128]{1,0:T(8,128)S(1)} %bitcast_select_fusion.1.hs_ref.keep_ref, f32[288,128]{1,0:T(8,128)S(1)} %fusion.26.rest_ref), custom_call_target="tpu_custom_call" | custom-call | bytes 6000000 | tf_op jit(solution)/shard_map/away_rest/pallas_call | solution.py:240
  156.7 10.0 %all-to-all-start.4 = ((f32[32,24,128]{2,1,0:T(8,128)}), f32[32,24,128]{2,1,0:T(8,128)S(1)}, u32[]{:S(2)}, u32[]{:S(2)}) async-start(f32[32,24,128]{2,1,0:T(8,128)} %bitcast.67), calls=%async_computation.4 | async-start | bytes 786432 | tf_op jit(solution)/shard_map/all_to_all | solution.py:487
  167.0 2.7 %collective-permute-start.21 = (f32[32,16,128]{2,1,0:T(8,128)S(1)}, f32[32,16,128]{2,1,0:T(8,128)S(1)}, u32[]{:S(2)}, u32[]{:S(2)}) collective-permute-start(f32[32,16,128]{2,1,0:T(8,128)S(1)} %all-to-all-done.3.refs_0_), channel_id=1, source_target_pairs={{0,6},{2,0},{4,2},{6,4},{1,7},{3,1},{5,3},{7,5},{8,14},{10,8},{12,... | collective-permute-start | bytes 786440 | tf_op jit(solution)/shard_map/ppermute | solution.py:421
  170.7 3.4 %collective-permute-start.18 = (f32[256,128]{1,0:T(8,128)S(1)}, f32[256,128]{1,0:T(8,128)S(1)}, u32[]{:S(2)}, u32[]{:S(2)}) collective-permute-start(f32[256,128]{1,0:T(8,128)S(1)} %add_select_fusion.5.late_ref), channel_id=1, source_target_pairs={{0,1},{1,0},{2,3},{3,2},{4,5},{5,4},{6,7},{7,6},{8,9},{9,8},{10,11... | collective-permute-start | bytes 393224 | tf_op jit(solution)/shard_map/ppermute | solution.py:421
  177.7 6.4 %all-to-all-done.4 = f32[32,24,128]{2,1,0:T(8,128)S(1)} async-done(((f32[32,24,128]{2,1,0:T(8,128)}), f32[32,24,128]{2,1,0:T(8,128)S(1)}, u32[]{:S(2)}, u32[]{:S(2)}) %all-to-all-start.4) | async-done | bytes 393248 | tf_op jit(solution)/shard_map/all_to_all | solution.py:487
  184.2 4.0 %collective-permute-start.23 = (f32[4,32,16,128]{3,2,1,0:T(8,128)S(1)}, f32[4,32,16,128]{3,2,1,0:T(8,128)S(1)}, u32[]{:S(2)}, u32[]{:S(2)}) collective-permute-start(f32[4,32,16,128]{3,2,1,0:T(8,128)S(1)} %join.2.piece_ref), channel_id=1, source_target_pairs={{0,1},{1,0},{2,3},{3,2},{4,5},{5,4},{6,7},{7,6},{8,9},{9,8},{10,11... | collective-permute-start | bytes 3145736 | tf_op jit(solution)/shard_map/ppermute | solution.py:421
  188.3 3.8 %patch_rows.1 = f32[8192,128]{1,0:T(8,128)S(1)} custom-call(s32[64]{0:T(128)S(1)} %pad_add_fusion.1.row_ref, s32[64]{0:T(128)S(1)} %pad_add_fusion.2.y_ref, f32[8192,128]{1,0:T(8,128)} %bitcast.140, f32[256,128]{1,0:T(8,128)S(1)} %bitcast.134, f32[768,128]{1,0:T(8,128)S(1)} %bitcast.126), custom_call_target="tpu_custom_call" | custom-call | bytes 12000000 | tf_op jit(solution)/shard_map/patch_rows/pallas_call | solution.py:264
  192.1 2.0 copy-done
  194.1 11.5 %factors.1 = (bf16[1024,1024]{1,0:T(8,128)(2,1)}, f32[512,512]{1,0:T(8,128)S(1)}) custom-call(s32[8]{0:T(128)S(1)} %stack.43.info_ref, s32[64]{0:T(128)S(1)} %pad_add_fusion.1.row_ref, s32[64]{0:T(128)S(1)} %pad_add_fusion.2.y_ref, f32[2048,128]{1,0:T(8,128)S(1)} %copy-done.2, f32[2048,128]{1,0:T(8,128)S(1)} %copy-done.4, ...), custom_call_target="tpu_custom_call" | custom-call | bytes 36000000 | tf_op jit(solution)/shard_map/factors/pallas_call | solution.py:363
  206.7 14.6 %update.1 = f32[512,16,128]{2,1,0:T(8,128)} custom-call(s32[8]{0:T(128)} %copy-done.9, f32[512,16,128]{2,1,0:T(8,128)} %bitcast.122, bf16[1024,1024]{1,0:T(8,128)(2,1)} %get-tuple-element.117.m_ref, f32[512,512]{1,0:T(8,128)} %copy-done.1, f32[8,4,4,128,128]{4,3,2,1,0:T(8,128)} %bitcast.142), custom_call_target="tpu_custom_call" | custom-call | bytes 30000000 | tf_op jit(solution)/shard_map/update/pallas_call | solution.py:394
  (108 shorter events, 22.9 us)
Async XLA Ops:
  24.7 17.9 %collective-permute-start = (f32[4,224,128]{2,1,0:T(8,128)}, f32[4,224,128]{2,1,0:T(8,128)}, u32[]{:S(2)}, u32[]{:S(2)}) collective-permute-start(f32[4,224,128]{2,1,0:T(8,128)} %bitcast.29), channel_id=1, source_target_pairs={{0,128},{8,136},{1,129},{9,137},{2,130},{10,138},{3,131},{11,139},... | collective-permute-start | bytes 1376264 | tf_op jit(solution)/shard_map/ppermute | solution.py:429
  30.3 22.8 %collective-permute-start.1 = (f32[4,224,128]{2,1,0:T(8,128)}, f32[4,224,128]{2,1,0:T(8,128)}, u32[]{:S(2)}, u32[]{:S(2)}) collective-permute-start(f32[4,224,128]{2,1,0:T(8,128)} %bitcast.30), channel_id=1, source_target_pairs={{0,64},{8,72},{1,65},{9,73},{2,66},{10,74},{3,67},{11,75},{4,68},{... | collective-permute-start | bytes 1376264 | tf_op jit(solution)/shard_map/ppermute | solution.py:429
  32.4 20.7 %collective-permute-start.2 = (f32[4,224,128]{2,1,0:T(8,128)}, f32[4,224,128]{2,1,0:T(8,128)}, u32[]{:S(2)}, u32[]{:S(2)}) collective-permute-start(f32[4,224,128]{2,1,0:T(8,128)} %bitcast.31), channel_id=1, source_target_pairs={{0,192},{8,200},{1,193},{9,201},{2,194},{10,202},{3,195},{11,203},... | collective-permute-start | bytes 1376264 | tf_op jit(solution)/shard_map/ppermute | solution.py:429
  34.5 31.8 %all-to-all-start = ((f32[32,32,128]{2,1,0:T(8,128)}), f32[32,32,128]{2,1,0:T(8,128)S(1)}, u32[]{:S(2)}, u32[]{:S(2)}) async-start(f32[32,32,128]{2,1,0:T(8,128)} %bitcast.38), calls=%async_computation | async-start | bytes 1048576 | tf_op jit(solution)/shard_map/all_to_all | solution.py:456
  39.9 103.8 %all-reduce.16.cloned.1.call-start = ((), (), s32[]{:S(2)}) async-start(), calls=%async_computation.9 | async-start | bytes 2097152 | tf_op jit(solution)/shard_map/psum | solution.py:461
  54.5 0.8 copy-start.14
  55.3 3.9 %collective-permute-start.3 = (f32[224,128]{1,0:T(8,128)S(1)}, f32[224,128]{1,0:T(8,128)S(1)}, u32[]{:S(2)}, u32[]{:S(2)}) collective-permute-start(f32[224,128]{1,0:T(8,128)S(1)} %get-tuple-element.216), channel_id=1, source_target_pairs={{0,32},{8,40},{64,96},{72,104},{128,160},{136,168},{192,224},{200,... | collective-permute-start | bytes 344072 | tf_op jit(solution)/shard_map/ppermute | solution.py:437
  56.6 6.8 %collective-permute-start.4 = (f32[224,128]{1,0:T(8,128)S(1)}, f32[224,128]{1,0:T(8,128)S(1)}, u32[]{:S(2)}, u32[]{:S(2)}) collective-permute-start(f32[224,128]{1,0:T(8,128)S(1)} %get-tuple-element.215), channel_id=1, source_target_pairs={{0,16},{8,24},{64,80},{72,88},{128,144},{136,152},{192,208},{200,2... | collective-permute-start | bytes 344072 | tf_op jit(solution)/shard_map/ppermute | solution.py:437
  57.9 5.5 %collective-permute-start.5 = (f32[224,128]{1,0:T(8,128)S(1)}, f32[224,128]{1,0:T(8,128)S(1)}, u32[]{:S(2)}, u32[]{:S(2)}) collective-permute-start(f32[224,128]{1,0:T(8,128)S(1)} %get-tuple-element.214), channel_id=1, source_target_pairs={{0,48},{8,56},{64,112},{72,120},{128,176},{136,184},{192,240},{200... | collective-permute-start | bytes 344072 | tf_op jit(solution)/shard_map/ppermute | solution.py:437
  65.1 141.6 %all-gather.3.cloned.1.call-start = ((), (), s32[]{:S(2)}) async-start(), calls=%async_computation.10 | async-start | bytes 9437184 | tf_op jit(solution)/shard_map/all_gather | solution.py:467
  67.5 13.8 %collective-permute-start.6 = (f32[4,128,128]{2,1,0:T(8,128)S(1)}, f32[4,128,128]{2,1,0:T(8,128)S(1)}, u32[]{:S(2)}, u32[]{:S(2)}) collective-permute-start(f32[4,128,128]{2,1,0:T(8,128)S(1)} %bitcast.127), channel_id=1, source_target_pairs={{0,64},{64,128},{128,192},{192,0},{1,65},{65,129},{129,193},{193,1... | collective-permute-start | bytes 786440 | tf_op jit(solution)/shard_map/ppermute | solution.py:421
  70.7 10.6 %collective-permute-start.7 = (f32[4,128,128]{2,1,0:T(8,128)S(1)}, f32[4,128,128]{2,1,0:T(8,128)S(1)}, u32[]{:S(2)}, u32[]{:S(2)}) collective-permute-start(f32[4,128,128]{2,1,0:T(8,128)S(1)} %bitcast.128), channel_id=1, source_target_pairs={{0,192},{64,0},{128,64},{192,128},{1,193},{65,1},{129,65},{193,129... | collective-permute-start | bytes 786440 | tf_op jit(solution)/shard_map/ppermute | solution.py:421
  70.7 10.8 %collective-permute-start.8 = (f32[4,128,128]{2,1,0:T(8,128)S(1)}, f32[4,128,128]{2,1,0:T(8,128)S(1)}, u32[]{:S(2)}, u32[]{:S(2)}) collective-permute-start(f32[4,128,128]{2,1,0:T(8,128)S(1)} %bitcast.129), channel_id=1, source_target_pairs={{0,128},{64,192},{128,0},{192,64},{1,129},{65,193},{129,1},{193,65... | collective-permute-start | bytes 786440 | tf_op jit(solution)/shard_map/ppermute | solution.py:421
  84.1 37.2 %collective-permute-start.10 = (f32[4,288,128]{2,1,0:T(8,128)}, f32[4,288,128]{2,1,0:T(8,128)}, u32[]{:S(2)}, u32[]{:S(2)}) collective-permute-start(f32[4,288,128]{2,1,0:T(8,128)} %get-tuple-element.205), channel_id=1, source_target_pairs={{0,64},{8,72},{1,65},{9,73},{2,66},{10,74},{3,67},{11,75},{4,68},{... | collective-permute-start | bytes 1769480 | tf_op jit(solution)/shard_map/ppermute | solution.py:429
  89.2 32.0 %collective-permute-start.11 = (f32[4,288,128]{2,1,0:T(8,128)}, f32[4,288,128]{2,1,0:T(8,128)}, u32[]{:S(2)}, u32[]{:S(2)}) collective-permute-start(f32[4,288,128]{2,1,0:T(8,128)} %get-tuple-element.204), channel_id=1, source_target_pairs={{0,192},{8,200},{1,193},{9,201},{2,194},{10,202},{3,195},{11,203},... | collective-permute-start | bytes 1769480 | tf_op jit(solution)/shard_map/ppermute | solution.py:429
  92.6 28.7 %collective-permute-start.9 = (f32[4,288,128]{2,1,0:T(8,128)}, f32[4,288,128]{2,1,0:T(8,128)}, u32[]{:S(2)}, u32[]{:S(2)}) collective-permute-start(f32[4,288,128]{2,1,0:T(8,128)} %get-tuple-element.206), channel_id=1, source_target_pairs={{0,128},{8,136},{1,129},{9,137},{2,130},{10,138},{3,131},{11,139},... | collective-permute-start | bytes 1769480 | tf_op jit(solution)/shard_map/ppermute | solution.py:429
  96.8 11.3 %all-to-all-start.1 = ((f32[8,16,128]{2,1,0:T(8,128)}), f32[8,16,128]{2,1,0:T(8,128)S(1)}, u32[]{:S(2)}, u32[]{:S(2)}) async-start(f32[8,16,128]{2,1,0:T(8,128)} %bitcast.40), calls=%async_computation.1 | async-start | bytes 131072 | tf_op jit(solution)/shard_map/all_to_all | solution.py:471
  108.0 13.2 %all-to-all-start.2 = ((f32[32,8,128]{2,1,0:T(8,128)}), f32[32,8,128]{2,1,0:T(8,128)S(1)}, u32[]{:S(2)}, u32[]{:S(2)}) async-start(f32[32,8,128]{2,1,0:T(8,128)} %bitcast.46), calls=%async_computation.2 | async-start | bytes 262144 | tf_op jit(solution)/shard_map/all_to_all | solution.py:469
  121.3 21.0 %collective-permute-start.12 = (f32[256,128]{1,0:T(8,128)S(1)}, f32[256,128]{1,0:T(8,128)S(1)}, u32[]{:S(2)}, u32[]{:S(2)}) collective-permute-start(f32[256,128]{1,0:T(8,128)S(1)} %bitcast.131), channel_id=1, source_target_pairs={{0,4},{1,5},{8,12},{9,13},{16,20},{17,21},{24,28},{25,29},{32,36},... | collective-permute-start | bytes 393224 | tf_op jit(solution)/shard_map/ppermute | solution.py:479
  124.9 18.8 %collective-permute-start.13 = (f32[256,128]{1,0:T(8,128)S(1)}, f32[256,128]{1,0:T(8,128)}, u32[]{:S(2)}, u32[]{:S(2)}) collective-permute-start(f32[256,128]{1,0:T(8,128)S(1)} %bitcast.132), channel_id=1, source_target_pairs={{0,2},{1,3},{8,10},{9,11},{16,18},{17,19},{24,26},{25,27},{32,34},... | collective-permute-start | bytes 393224 | tf_op jit(solution)/shard_map/ppermute | solution.py:479
  127.5 25.8 %all-to-all-start.3 = ((f32[32,16,128]{2,1,0:T(8,128)}), f32[32,16,128]{2,1,0:T(8,128)S(1)}, u32[]{:S(2)}, u32[]{:S(2)}) async-start(f32[32,16,128]{2,1,0:T(8,128)} %broadcast_in_dim.281), calls=%async_computation.3 | async-start | bytes 524288 | tf_op jit(solution)/shard_map/all_to_all | solution.py:477
  133.6 8.8 %copy-start.13 = (f32[4,288,128]{2,1,0:T(8,128)}, f32[4,288,128]{2,1,0:T(8,128)S(1)}, u32[]{:S(2)}) copy-start(f32[4,288,128]{2,1,0:T(8,128)S(1)} %bitcast_select_fusion) | copy-start | bytes 1769476
  133.6 13.4 %collective-permute-start.15 = (f32[288,128]{1,0:T(8,128)S(1)}, f32[288,128]{1,0:T(8,128)S(1)}, u32[]{:S(2)}, u32[]{:S(2)}) collective-permute-start(f32[288,128]{1,0:T(8,128)S(1)} %get-tuple-element.213), channel_id=1, source_target_pairs={{0,32},{8,40},{64,96},{72,104},{128,160},{136,168},{192,224},{200,... | collective-permute-start | bytes 442376 | tf_op jit(solution)/shard_map/ppermute | solution.py:437
  139.7 11.6 %collective-permute-start.16 = (f32[288,128]{1,0:T(8,128)S(1)}, f32[288,128]{1,0:T(8,128)S(1)}, u32[]{:S(2)}, u32[]{:S(2)}) collective-permute-start(f32[288,128]{1,0:T(8,128)S(1)} %get-tuple-element.212), channel_id=1, source_target_pairs={{0,16},{8,24},{64,80},{72,88},{128,144},{136,152},{192,208},{200,2... | collective-permute-start | bytes 442376 | tf_op jit(solution)/shard_map/ppermute | solution.py:437
  141.0 12.3 %collective-permute-start.17 = (f32[288,128]{1,0:T(8,128)S(1)}, f32[288,128]{1,0:T(8,128)S(1)}, u32[]{:S(2)}, u32[]{:S(2)}) collective-permute-start(f32[288,128]{1,0:T(8,128)S(1)} %get-tuple-element.211), channel_id=1, source_target_pairs={{0,48},{8,56},{64,112},{72,120},{128,176},{136,184},{192,240},{200... | collective-permute-start | bytes 442376 | tf_op jit(solution)/shard_map/ppermute | solution.py:437
  142.3 4.0 %collective-permute-start.14 = (f32[256,128]{1,0:T(8,128)S(1)}, f32[256,128]{1,0:T(8,128)S(1)}, u32[]{:S(2)}, u32[]{:S(2)}) collective-permute-start(f32[256,128]{1,0:T(8,128)S(1)} %bitcast.133), channel_id=1, source_target_pairs={{0,6},{1,7},{8,14},{9,15},{16,22},{17,23},{24,30},{25,31},{32,38},... | collective-permute-start | bytes 393224 | tf_op jit(solution)/shard_map/ppermute | solution.py:479
  143.7 33.1 %collective-permute-start.19 = (f32[2048,128]{1,0:T(8,128)}, f32[2048,128]{1,0:T(8,128)S(1)}, u32[]{:S(2)}, u32[]{:S(2)}) collective-permute-start(f32[2048,128]{1,0:T(8,128)} %all-reduce.16.cloned.1.call-done.own_ref), channel_id=1, source_target_pairs={{0,1},{1,0},{2,3},{3,2},{4,5},{5,4},{6,7},{7,6},{8,9},{9,8},{10,11... | collective-permute-start | bytes 3145736 | tf_op jit(solution)/shard_map/ppermute | solution.py:421
  146.4 20.4 %copy-start.15 = (f32[256,128]{1,0:T(8,128)}, f32[256,128]{1,0:T(8,128)S(1)}, u32[]{:S(2)}) copy-start(f32[256,128]{1,0:T(8,128)S(1)} %collective-permute-done.14) | copy-start | bytes 393220
  156.7 27.4 %all-to-all-start.4 = ((f32[32,24,128]{2,1,0:T(8,128)}), f32[32,24,128]{2,1,0:T(8,128)S(1)}, u32[]{:S(2)}, u32[]{:S(2)}) async-start(f32[32,24,128]{2,1,0:T(8,128)} %bitcast.67), calls=%async_computation.4 | async-start | bytes 786432 | tf_op jit(solution)/shard_map/all_to_all | solution.py:487
  166.8 9.0 %collective-permute-start.20 = (f32[32,16,128]{2,1,0:T(8,128)S(1)}, f32[32,16,128]{2,1,0:T(8,128)S(1)}, u32[]{:S(2)}, u32[]{:S(2)}) collective-permute-start(f32[32,16,128]{2,1,0:T(8,128)S(1)} %all-to-all-done.3.refs_0_), channel_id=1, source_target_pairs={{0,2},{2,4},{4,6},{6,0},{1,3},{3,5},{5,7},{7,1},{8,10},{10,12},{12... | collective-permute-start | bytes 786440 | tf_op jit(solution)/shard_map/ppermute | solution.py:421
  167.0 8.7 %collective-permute-start.21 = (f32[32,16,128]{2,1,0:T(8,128)S(1)}, f32[32,16,128]{2,1,0:T(8,128)S(1)}, u32[]{:S(2)}, u32[]{:S(2)}) collective-permute-start(f32[32,16,128]{2,1,0:T(8,128)S(1)} %all-to-all-done.3.refs_0_), channel_id=1, source_target_pairs={{0,6},{2,0},{4,2},{6,4},{1,7},{3,1},{5,3},{7,5},{8,14},{10,8},{12,... | collective-permute-start | bytes 786440 | tf_op jit(solution)/shard_map/ppermute | solution.py:421
  169.7 7.1 %collective-permute-start.22 = (f32[32,16,128]{2,1,0:T(8,128)S(1)}, f32[32,16,128]{2,1,0:T(8,128)S(1)}, u32[]{:S(2)}, u32[]{:S(2)}) collective-permute-start(f32[32,16,128]{2,1,0:T(8,128)S(1)} %all-to-all-done.3.refs_0_), channel_id=1, source_target_pairs={{0,4},{2,6},{4,0},{6,2},{1,5},{3,7},{5,1},{7,3},{8,12},{10,14},{12... | collective-permute-start | bytes 786440 | tf_op jit(solution)/shard_map/ppermute | solution.py:421
  170.7 4.4 %collective-permute-start.18 = (f32[256,128]{1,0:T(8,128)S(1)}, f32[256,128]{1,0:T(8,128)S(1)}, u32[]{:S(2)}, u32[]{:S(2)}) collective-permute-start(f32[256,128]{1,0:T(8,128)S(1)} %add_select_fusion.5.late_ref), channel_id=1, source_target_pairs={{0,1},{1,0},{2,3},{3,2},{4,5},{5,4},{6,7},{7,6},{8,9},{9,8},{10,11... | collective-permute-start | bytes 393224 | tf_op jit(solution)/shard_map/ppermute | solution.py:421
  175.1 0.6 copy-start.7
  176.8 1.0 copy-start.3
  184.2 9.9 %collective-permute-start.23 = (f32[4,32,16,128]{3,2,1,0:T(8,128)S(1)}, f32[4,32,16,128]{3,2,1,0:T(8,128)S(1)}, u32[]{:S(2)}, u32[]{:S(2)}) collective-permute-start(f32[4,32,16,128]{3,2,1,0:T(8,128)S(1)} %join.2.piece_ref), channel_id=1, source_target_pairs={{0,1},{1,0},{2,3},{3,2},{4,5},{5,4},{6,7},{7,6},{8,9},{9,8},{10,11... | collective-permute-start | bytes 3145736 | tf_op jit(solution)/shard_map/ppermute | solution.py:421
  188.2 5.9 %copy-start.9 = (s32[8]{0:T(128)}, s32[8]{0:T(128)S(1)}, u32[]{:S(2)}) copy-start(s32[8]{0:T(128)S(1)} %stack.43.info_ref) | copy-start | bytes 100
  188.2 5.9 %copy-start.2 = (f32[2048,128]{1,0:T(8,128)S(1)}, f32[2048,128]{1,0:T(8,128)}, u32[]{:S(2)}) copy-start(f32[2048,128]{1,0:T(8,128)} %all-reduce.16.cloned.1.call-done.own_ref) | copy-start | bytes 3145732
  188.2 5.9 %copy-start.4 = (f32[2048,128]{1,0:T(8,128)S(1)}, f32[2048,128]{1,0:T(8,128)}, u32[]{:S(2)}) copy-start(f32[2048,128]{1,0:T(8,128)} %copy-done.3) | copy-start | bytes 3145732
  188.2 5.9 %copy-start.5 = (s32[512,128]{1,0:T(8,128)S(1)}, s32[512,128]{1,0:T(8,128)}, u32[]{:S(2)}) copy-start(s32[512,128]{1,0:T(8,128)} %broadcast_in_dim.270.spot0_ref) | copy-start | bytes 786436
  188.2 5.9 %copy-start.6 = (s32[512,128]{1,0:T(8,128)S(1)}, s32[512,128]{1,0:T(8,128)}, u32[]{:S(2)}) copy-start(s32[512,128]{1,0:T(8,128)} %broadcast_in_dim.271.spot1_ref) | copy-start | bytes 786436
  188.3 5.9 %copy-start.8 = (f32[256,128]{1,0:T(8,128)S(1)}, f32[256,128]{1,0:T(8,128)}, u32[]{:S(2)}) copy-start(f32[256,128]{1,0:T(8,128)} %copy-done.7) | copy-start | bytes 393220
  188.3 5.9 %copy-start.11 = (f32[2,512,512]{2,1,0:T(8,128)S(1)}, f32[2,512,512]{2,1,0:T(8,128)}, u32[]{:S(2)}) copy-start(f32[2,512,512]{2,1,0:T(8,128)} %inv_ref.1) | copy-start | bytes 6291460
  192.1 2.0 copy-start
  194.1 12.6 %copy-start.16 = (s32[2,512]{1,0:T(2,128)S(1)}, s32[2,512]{1,0:T(2,128)}, u32[]{:S(2)}) copy-start(s32[2,512]{1,0:T(2,128)} %param.12) | copy-start | bytes 12292
  205.7 1.0 copy-start.1
Sparse Core Ops, SparseCore 0:
  65.2 52.2 all-reduce.15
Sparse Core Ops, SparseCore 1:
  82.6 118.6 all-gather.2
